TPU v7x, 32 devices: a whole 2x2x4 slice. The times are simulated.
32 devices in a mesh: dp: 8 (over z, y), tensor: 4 (over x, core).
Axes of the slice: x: 2, y: 2, z: 4, core: 2. Of those that a mesh axis runs over, the one named last changes fastest.
Arguments:
- tokens: bfloat16 [8192, 2048], P('dp'), may hold values from -6 to 6
- attention_gain: float32 [2048], replicated, may hold values from 0.5 to 1.5
- query_weight: bfloat16 [2048, 2048], P(None, 'tensor'), may hold values from -0.125 to 0.125
- key_weight: bfloat16 [2048, 1024], P(None, 'tensor'), may hold values from -0.125 to 0.125
- value_weight: bfloat16 [2048, 1024], P(None, 'tensor'), may hold values from -0.125 to 0.125
- query_gain: float32 [128], replicated, may hold values from 0.25 to 1.75
- key_gain: float32 [128], replicated, may hold values from 0.25 to 1.75
- output_weight: bfloat16 [2048, 2048], P('tensor'), may hold values from -1 to 1
- feedforward_gain: float32 [2048], replicated, may hold values from 0.5 to 1.5
- gate_weight: bfloat16 [2048, 6144], P(None, 'tensor'), may hold values from -0.125 to 0.125
- up_weight: bfloat16 [2048, 6144], P(None, 'tensor'), may hold values from -0.125 to 0.125
- down_weight: bfloat16 [6144, 2048], P('tensor'), may hold values from -0.078125 to 0.078125
- segment_numbers: int32 [8192], P('dp'), may hold values from 0 to 3, as said below
- positions: int32 [8192], P('dp'), may hold values from 0 to 2047, as said below
- cotangent: bfloat16 [8192, 2048], P('dp'), may hold values from -6 to 6
Outputs:
- layer_output: bfloat16 [8192, 2048], P('dp')
- tokens_gradient: bfloat16 [8192, 2048], P('dp')
- attention_gain_gradient: float32 [2048], P('dp')
- query_gradient: float32 [2048, 2048], P('dp', 'tensor')
- key_gradient: float32 [2048, 1024], P('dp', 'tensor')
- value_gradient: float32 [2048, 1024], P('dp', 'tensor')
- query_gain_gradient: float32 [128], P('dp')
- key_gain_gradient: float32 [128], P('dp')
- output_gradient: float32 [2048, 2048], P('tensor', 'dp')
- feedforward_gain_gradient: float32 [2048], P('dp')
- gate_gradient: float32 [2048, 6144], P('dp', 'tensor')
- up_gradient: float32 [2048, 6144], P('dp', 'tensor')
- down_gradient: float32 [6144, 2048], P('tensor', 'dp')
Inputs may be any that keep to these rules, and one draw needn't show every extreme that they name: `segment_numbers`: each aligned sequence of 1024 tokens holds four documents numbered 0 to 3 in order, never falling, each of 128 tokens or more. `positions`: within a document the position rises by one from token to token; only the first document of a sequence may start at a position above 0, the others start at 0.
All inputs are finite; a program needn't handle non-finite values.
Results may differ from a plain program's by a relative error of at most 0.014.
Values sent between devices are 32-bit elements; how exact they have to be, the bound alone decides.
A program may use at most 256 MiB of HBM per device.

v0:
```python
import jax
import jax.numpy as jnp
from jax import lax
from jax.sharding import PartitionSpec as P

HD = 128
SEQ_LEN = 1024


epsilon = 1e-06
rope_base = 1000000.0
masked = -1e30


def rms_inverse(value):
    return lax.rsqrt(jnp.mean(value * value, axis=-1, keepdims=True) + epsilon)


def norm_back(upstream, value, inverse, gain):
    scaled = upstream * gain
    return inverse * scaled - value * inverse**3 * jnp.mean(scaled * value, axis=-1, keepdims=True)


def rotary_tables(positions):
    exponent = jnp.arange(0, HD, 2, dtype=jnp.float32) / HD
    frequency = rope_base ** (-exponent)
    phase = positions.astype(jnp.float32)[:, None] * frequency[None, :]
    phase = jnp.concatenate([phase, phase], axis=-1)
    return (jnp.cos(phase), jnp.sin(phase))


def rotate(value, cosine, sine):
    half = value.shape[-1] // 2
    turned = jnp.concatenate([-value[..., half:], value[..., :half]], axis=-1)
    return value * cosine + turned * sine


def rotate_back(upstream, cosine, sine):
    half = upstream.shape[-1] // 2
    moved = upstream * sine
    return upstream * cosine + jnp.concatenate([moved[..., half:], -moved[..., :half]], axis=-1)


def block_scores(query_rows, keys, row_segments, segments, begin):
    scores = jnp.einsum(
        "rkgd,tkd->kgrt", query_rows, keys, preferred_element_type=jnp.float32
    ) * HD ** (-0.5)
    rows = begin + lax.iota(jnp.int32, query_rows.shape[0])
    columns = lax.iota(jnp.int32, keys.shape[0])
    allowed = (row_segments[:, None] == segments[None, :]) & (rows[:, None] >= columns[None, :])
    return jnp.where(allowed[None, None], scores, masked)


def attend(item):
    queries, keys, values, segments = item
    length = queries.shape[0]
    width = min(512, length)
    outputs = []
    totals = []
    for begin in range(0, length, width):
        scores = block_scores(
            queries[begin : begin + width], keys, segments[begin : begin + width], segments, begin
        )
        peak = jnp.max(scores, axis=-1, keepdims=True)
        expons = jnp.exp(scores - peak)
        total = jnp.sum(expons, axis=-1, keepdims=True)
        chance_low = (expons / total).astype(jnp.bfloat16)
        outputs.append(
            jnp.einsum("kgrt,tkd->rkgd", chance_low, values, preferred_element_type=jnp.float32)
        )
        totals.append(peak + jnp.log(total))
    return (jnp.concatenate(outputs, axis=0), jnp.concatenate(totals, axis=2))


def attend_back(item):
    queries, keys, values, segments, totals, upstream = item
    length = queries.shape[0]
    width = min(512, length)
    query_parts = []
    key_grad = jnp.zeros(keys.shape, jnp.float32)
    value_grad = jnp.zeros(values.shape, jnp.float32)
    for begin in range(0, length, width):
        rows = queries[begin : begin + width]
        scores = block_scores(rows, keys, segments[begin : begin + width], segments, begin)
        chance = jnp.exp(scores - totals[:, :, begin : begin + width])
        chance_low = chance.astype(jnp.bfloat16)
        incoming = upstream[begin : begin + width]
        value_grad = value_grad + jnp.einsum(
            "kgrt,rkgd->tkd", chance_low, incoming, preferred_element_type=jnp.float32
        )
        along = jnp.einsum("rkgd,tkd->kgrt", incoming, values, preferred_element_type=jnp.float32)
        center = jnp.sum(along * chance, axis=-1, keepdims=True)
        score_grad = (chance * (along - center)).astype(jnp.bfloat16)
        query_parts.append(
            jnp.einsum("kgrt,tkd->rkgd", score_grad, keys, preferred_element_type=jnp.float32)
            * HD ** (-0.5)
        )
        key_grad = key_grad + jnp.einsum(
            "kgrt,rkgd->tkd", score_grad, rows, preferred_element_type=jnp.float32
        ) * HD ** (-0.5)
    return (jnp.concatenate(query_parts, axis=0), key_grad, value_grad)


def shards(
    tokens,
    attention_gain,
    query_weight,
    key_weight,
    value_weight,
    query_gain,
    key_gain,
    output_weight,
    feedforward_gain,
    gate_weight,
    up_weight,
    down_weight,
    segment_numbers,
    positions,
    cotangent,
):
    count = tokens.shape[0]
    batch = count // SEQ_LEN
    query_heads = query_weight.shape[1] // HD
    value_heads = key_weight.shape[1] // HD
    group = query_heads // value_heads
    inputs = tokens.astype(jnp.float32)
    first_inverse = rms_inverse(inputs)
    first_normed = inputs * first_inverse
    normed_low = (first_normed * attention_gain).astype(jnp.bfloat16)
    query_raw = jnp.dot(normed_low, query_weight, preferred_element_type=jnp.float32).reshape(
        count, query_heads, HD
    )
    key_raw = jnp.dot(normed_low, key_weight, preferred_element_type=jnp.float32).reshape(
        count, value_heads, HD
    )
    value_low = jnp.dot(normed_low, value_weight, preferred_element_type=jnp.float32).astype(
        jnp.bfloat16
    )
    cosine, sine = rotary_tables(positions)
    cosine = cosine[:, None]
    sine = sine[:, None]
    query_inverse = rms_inverse(query_raw)
    query_unit = query_raw * query_inverse
    query_low = rotate(query_unit * query_gain, cosine, sine).astype(jnp.bfloat16)
    key_inverse = rms_inverse(key_raw)
    key_unit = key_raw * key_inverse
    key_low = rotate(key_unit * key_gain, cosine, sine).astype(jnp.bfloat16)
    queries = query_low.reshape(batch, SEQ_LEN, value_heads, group, HD)
    keys = key_low.reshape(batch, SEQ_LEN, value_heads, HD)
    values = value_low.reshape(batch, SEQ_LEN, value_heads, HD)
    segments = segment_numbers.reshape(batch, SEQ_LEN)
    mixed, totals = lax.map(attend, (queries, keys, values, segments))
    mixed_low = mixed.reshape(count, query_heads * HD).astype(jnp.bfloat16)
    attention = lax.psum(
        jnp.dot(mixed_low, output_weight, preferred_element_type=jnp.float32), "tensor"
    )
    hidden = inputs + attention
    second_inverse = rms_inverse(hidden)
    second_normed = hidden * second_inverse
    second_low = (second_normed * feedforward_gain).astype(jnp.bfloat16)
    gate = jnp.dot(second_low, gate_weight, preferred_element_type=jnp.float32)
    upward = jnp.dot(second_low, up_weight, preferred_element_type=jnp.float32)
    sigmoid_gate = jax.nn.sigmoid(gate)
    activated = gate * sigmoid_gate
    product_low = (activated * upward).astype(jnp.bfloat16)
    feedforward = lax.psum(
        jnp.dot(product_low, down_weight, preferred_element_type=jnp.float32), "tensor"
    )
    layer_output = (hidden + feedforward).astype(jnp.bfloat16)
    down_grad = jnp.einsum("tf,td->fd", product_low, cotangent, preferred_element_type=jnp.float32)
    product_grad = jnp.einsum(
        "td,fd->tf", cotangent, down_weight, preferred_element_type=jnp.float32
    )
    gate_grad_low = (
        product_grad * upward * sigmoid_gate * (1.0 + gate * (1.0 - sigmoid_gate))
    ).astype(jnp.bfloat16)
    upward_grad_low = (product_grad * activated).astype(jnp.bfloat16)
    gate_weight_grad = jnp.einsum(
        "td,tf->df", second_low, gate_grad_low, preferred_element_type=jnp.float32
    )
    upward_weight_grad = jnp.einsum(
        "td,tf->df", second_low, upward_grad_low, preferred_element_type=jnp.float32
    )
    second_part = jnp.einsum(
        "tf,df->td", gate_grad_low, gate_weight, preferred_element_type=jnp.float32
    )
    second_part = second_part + jnp.einsum(
        "tf,df->td", upward_grad_low, up_weight, preferred_element_type=jnp.float32
    )
    second_grad = lax.psum(second_part, "tensor")
    second_gain_grad = jnp.sum(second_grad * second_normed, axis=0)
    hidden_grad = cotangent.astype(jnp.float32) + norm_back(
        second_grad, hidden, second_inverse, feedforward_gain
    )
    hidden_low = hidden_grad.astype(jnp.bfloat16)
    output_weight_grad = jnp.einsum(
        "tc,td->cd", mixed_low, hidden_low, preferred_element_type=jnp.float32
    )
    mixed_grad = jnp.einsum(
        "td,cd->tc", hidden_low, output_weight, preferred_element_type=jnp.float32
    ).astype(jnp.bfloat16)
    upstream = mixed_grad.reshape(batch, SEQ_LEN, value_heads, group, HD)
    query_back, key_back, value_back = lax.map(
        attend_back, (queries, keys, values, segments, totals, upstream)
    )
    query_unit_grad = rotate_back(query_back.reshape(count, query_heads, HD), cosine, sine)
    key_unit_grad = rotate_back(key_back.reshape(count, value_heads, HD), cosine, sine)
    query_gain_part = jnp.sum(query_unit_grad * query_unit, axis=(0, 1))
    key_gain_part = jnp.sum(key_unit_grad * key_unit, axis=(0, 1))
    query_raw_grad = (
        norm_back(query_unit_grad, query_raw, query_inverse, query_gain)
        .reshape(count, query_heads * HD)
        .astype(jnp.bfloat16)
    )
    key_raw_grad = (
        norm_back(key_unit_grad, key_raw, key_inverse, key_gain)
        .reshape(count, value_heads * HD)
        .astype(jnp.bfloat16)
    )
    value_raw_grad = value_back.reshape(count, value_heads * HD).astype(jnp.bfloat16)
    query_weight_grad = jnp.einsum(
        "td,tc->dc", normed_low, query_raw_grad, preferred_element_type=jnp.float32
    )
    key_weight_grad = jnp.einsum(
        "td,tc->dc", normed_low, key_raw_grad, preferred_element_type=jnp.float32
    )
    value_weight_grad = jnp.einsum(
        "td,tc->dc", normed_low, value_raw_grad, preferred_element_type=jnp.float32
    )
    first_part = jnp.einsum(
        "tc,dc->td", query_raw_grad, query_weight, preferred_element_type=jnp.float32
    )
    first_part = first_part + jnp.einsum(
        "tc,dc->td", key_raw_grad, key_weight, preferred_element_type=jnp.float32
    )
    first_part = first_part + jnp.einsum(
        "tc,dc->td", value_raw_grad, value_weight, preferred_element_type=jnp.float32
    )
    first_grad, query_gain_grad, key_gain_grad = lax.psum(
        (first_part, query_gain_part, key_gain_part), "tensor"
    )
    first_gain_grad = jnp.sum(first_grad * first_normed, axis=0)
    tokens_gradient = (
        hidden_grad + norm_back(first_grad, inputs, first_inverse, attention_gain)
    ).astype(jnp.bfloat16)
    summed = (
        lax.psum_scatter(first_gain_grad, "dp", scatter_dimension=0, tiled=True),
        lax.psum_scatter(query_weight_grad, "dp", scatter_dimension=0, tiled=True),
        lax.psum_scatter(key_weight_grad, "dp", scatter_dimension=0, tiled=True),
        lax.psum_scatter(value_weight_grad, "dp", scatter_dimension=0, tiled=True),
        lax.psum_scatter(query_gain_grad, "dp", scatter_dimension=0, tiled=True),
        lax.psum_scatter(key_gain_grad, "dp", scatter_dimension=0, tiled=True),
        lax.psum_scatter(output_weight_grad, "dp", scatter_dimension=1, tiled=True),
        lax.psum_scatter(second_gain_grad, "dp", scatter_dimension=0, tiled=True),
        lax.psum_scatter(gate_weight_grad, "dp", scatter_dimension=0, tiled=True),
        lax.psum_scatter(upward_weight_grad, "dp", scatter_dimension=0, tiled=True),
        lax.psum_scatter(down_grad, "dp", scatter_dimension=1, tiled=True),
    )
    return (
        layer_output,
        tokens_gradient,
        summed[0],
        summed[1],
        summed[2],
        summed[3],
        summed[4],
        summed[5],
        summed[6],
        summed[7],
        summed[8],
        summed[9],
        summed[10],
    )


def solution(mesh):
    return jax.shard_map(
        shards,
        mesh=mesh,
        in_specs=(
            P("dp", None),
            P(),
            P(None, "tensor"),
            P(None, "tensor"),
            P(None, "tensor"),
            P(),
            P(),
            P("tensor", None),
            P(),
            P(None, "tensor"),
            P(None, "tensor"),
            P("tensor", None),
            P("dp"),
            P("dp"),
            P("dp", None),
        ),
        out_specs=(
            P("dp", None),
            P("dp", None),
            P("dp"),
            P("dp", "tensor"),
            P("dp", "tensor"),
            P("dp", "tensor"),
            P("dp"),
            P("dp"),
            P("tensor", "dp"),
            P("dp"),
            P("dp", "tensor"),
            P("dp", "tensor"),
            P("tensor", "dp"),
        ),
        check_vma=False,
    )
```

profile of v0, /device:TPU:24, one launch (start us, length us, event | category | flops | bytes accessed | tf_op | source)
XLA Modules:
  0.0 1737.0 jit_solution(6786828571488381660)
XLA Ops:
  46.9 153.9 %all-reduce.11.cloned.1.call-done = f32[1024,2048]{1,0:T(8,128)} async-done(((f32[1024,2048]{1,0:T(8,128)}), f32[1024,2048]{1,0:T(8,128)}) %all-reduce.11.cloned.1.call-update) | async-done | bytes 8388624 | tf_op jit(solution)/shard_map/psum | solution.py:154
  209.8 12.0 fusion.84
  221.7 10.6 fusion.83
  232.4 15.3 multiply_convert_fusion.1
  247.7 10.0 fusion.86
  257.7 11.3 convolution_add_fusion
  269.2 11.7 fusion.85
  281.0 141.3 %all-reduce.13.cloned.1.call-done = f32[1024,2048]{1,0:T(8,128)} async-done(((f32[1024,2048]{1,0:T(8,128)}), f32[1024,2048]{1,0:T(8,128)}) %all-reduce.13.cloned.1.call-update) | async-done | bytes 8388624 | tf_op jit(solution)/shard_map/psum | solution.py:190
  422.3 7.1 multiply_reduce_fusion
  429.4 7.2 subtract_add_fusion
  494.8 8.2 fusion.42
  510.8 12.3 fusion.94
  523.6 12.5 fusion.93
  536.2 12.9 fusion.92
  551.6 221.3 %all-reduce.15.cloned.1.call-done = (f32[1024,2048]{1,0:T(8,128)}, f32[1024,2048]{1,0:T(8,128)}) async-done(((f32[1024,2048]{1,0:T(8,128)}, f32[1024,2048]{1,0:T(8,128)}), (f32[1024,2048]{1,0:T(8,128)}, f32[1024,2048]{1,0:T(8,128)})) %all-reduce.15.cloned.1.call-update) | async-done | bytes 16777232 | tf_op jit(solution)/shard_map/psum | solution.py:166
  779.1 32.8 %all-reduce.4 = (f32[2048]{0:T(1024)S(1)}, f32[128]{0:T(128)S(1)}, f32[128]{0:T(128)S(1)}, f32[2048]{0:T(1024)S(1)}) all-reduce(f32[2048]{0:T(1024)S(1)} %get-tuple-element.56, f32[128]{0:T(128)S(1)} %reduce_sum.170, f32[128]{0:T(128)S(1)} %get-tuple-element.68, ...), channel_id=2, replica_groups=mesh['dp'=8,'tensor'=4] {'dp'}, use_global_device_ids=true, to_apply=%region_19.20.clone | all-reduce | flops 4352 | bytes 34816
  819.6 9.5 add_convert_fusion
  829.0 9.0 fusion.8
  843.3 70.6 %reduce-scatter.10.cloned.1.call-done = f32[256,256]{1,0:T(8,128)} async-done(((f32[2048,256]{1,0:T(8,128)}), f32[256,256]{1,0:T(8,128)}) %reduce-scatter.10.cloned.1.call-update) | async-done | bytes 262160 | tf_op jit(solution)/shard_map/reduce_scatter | solution.py:249
  913.9 91.7 %reduce-scatter.14.cloned.1.call-done = f32[512,256]{1,0:T(8,128)} async-done(((f32[512,2048]{1,0:T(8,128)}), f32[512,256]{1,0:T(8,128)}) %reduce-scatter.14.cloned.1.call-update) | async-done | bytes 524304 | tf_op jit(solution)/shard_map/reduce_scatter | solution.py:253
  1005.6 92.5 %reduce-scatter.8.cloned.1.call-done = f32[256,512]{1,0:T(8,128)} async-done(((f32[2048,512]{1,0:T(8,128)}), f32[256,512]{1,0:T(8,128)}) %reduce-scatter.8.cloned.1.call-update) | async-done | bytes 524304 | tf_op jit(solution)/shard_map/reduce_scatter | solution.py:248
  1098.1 210.7 %reduce-scatter.20.cloned.1.call-done = f32[1536,256]{1,0:T(8,128)} async-done(((f32[1536,2048]{1,0:T(8,128)}), f32[1536,256]{1,0:T(8,128)}) %reduce-scatter.20.cloned.1.call-update) | async-done | bytes 1572880 | tf_op jit(solution)/shard_map/reduce_scatter | solution.py:257
  1308.8 210.6 %reduce-scatter.18.cloned.1.call-done = f32[256,1536]{1,0:T(8,128)} async-done(((f32[2048,1536]{1,0:T(8,128)}), f32[256,1536]{1,0:T(8,128)}) %reduce-scatter.18.cloned.1.call-update) | async-done | bytes 1572880 | tf_op jit(solution)/shard_map/reduce_scatter | solution.py:256
  1519.5 210.5 %reduce-scatter.16.cloned.1.call-done = f32[256,1536]{1,0:T(8,128)} async-done(((f32[2048,1536]{1,0:T(8,128)}), f32[256,1536]{1,0:T(8,128)}) %reduce-scatter.16.cloned.1.call-update) | async-done | bytes 1572880 | tf_op jit(solution)/shard_map/reduce_scatter | solution.py:255
  (202 shorter events, 134.9 us)
Async XLA Ops:
  7.2 13.1 copy-start
  7.2 193.6 %all-reduce.11.cloned.1.call-start = ((), (), s32[]{:S(2)}) async-start(), calls=%async_computation.7 | async-start | bytes 16777216 | tf_op jit(solution)/shard_map/psum | solution.py:154
  14.3 10.8 copy-start.11
  14.3 10.8 copy-start.13
  46.8 159.8 %copy-start.32 = (f32[2048]{0:T(1024)S(1)}, f32[2048]{0:T(1024)}, u32[]{:S(2)}) copy-start(f32[2048]{0:T(1024)} %param.23) | copy-start | bytes 24580
  46.8 375.4 %all-reduce.13.cloned.1.call-start = ((), (), s32[]{:S(2)}) async-start(), calls=%async_computation.8 | async-start | bytes 16777216 | tf_op jit(solution)/shard_map/psum | solution.py:190
  209.8 12.0 copy-start.21
  221.7 10.6 copy-start.19
  247.7 10.0 copy-start.46
  247.7 10.0 copy-start.47
  269.1 503.8 %all-reduce.15.cloned.1.call-start = ((), (), s32[]{:S(2)}) async-start(), calls=%async_computation.16 | async-start | bytes 33554432 | tf_op jit(solution)/shard_map/psum | solution.py:166
  429.4 13.0 slice-start
  429.4 13.0 slice-start.1
  442.4 12.0 slice-start.2
  483.8 359.6 %reduce-scatter.12.cloned.1.call-start = ((), (), s32[]{:S(2)}) async-start(), calls=%async_computation.11 | async-start | bytes 2359296 | tf_op jit(solution)/shard_map/reduce_scatter | solution.py:250
  488.6 425.2 %reduce-scatter.10.cloned.1.call-start = ((), (), s32[]{:S(2)}) async-start(), calls=%async_computation.10 | async-start | bytes 2359296 | tf_op jit(solution)/shard_map/reduce_scatter | solution.py:249
  494.7 510.9 %reduce-scatter.14.cloned.1.call-start = ((), (), s32[]{:S(2)}) async-start(), calls=%async_computation.12 | async-start | bytes 4718592 | tf_op jit(solution)/shard_map/reduce_scatter | solution.py:253
  503.0 595.1 %reduce-scatter.8.cloned.1.call-start = ((), (), s32[]{:S(2)}) async-start(), calls=%async_computation.9 | async-start | bytes 4718592 | tf_op jit(solution)/shard_map/reduce_scatter | solution.py:248
  510.8 798.0 %reduce-scatter.20.cloned.1.call-start = ((), (), s32[]{:S(2)}) async-start(), calls=%async_computation.15 | async-start | bytes 14155776 | tf_op jit(solution)/shard_map/reduce_scatter | solution.py:257
  523.2 996.3 %reduce-scatter.18.cloned.1.call-start = ((), (), s32[]{:S(2)}) async-start(), calls=%async_computation.14 | async-start | bytes 14155776 | tf_op jit(solution)/shard_map/reduce_scatter | solution.py:256
  536.1 1193.8 %reduce-scatter.16.cloned.1.call-start = ((), (), s32[]{:S(2)}) async-start(), calls=%async_computation.13 | async-start | bytes 14155776 | tf_op jit(solution)/shard_map/reduce_scatter | solution.py:255
  549.0 223.8 %copy-start.34 = (f32[2048]{0:T(1024)S(1)}, f32[2048]{0:T(1024)}, u32[]{:S(2)}) copy-start(f32[2048]{0:T(1024)} %param.16) | copy-start | bytes 24580
  549.0 223.9 %copy-start.36 = (f32[1024]{0:T(1024)S(1)}, f32[1024]{0:T(1024)}, u32[]{:S(2)}) copy-start(f32[1024]{0:T(1024)} %copy-done.35) | copy-start | bytes 12292
  819.5 9.5 copy-start.39
  (38 other events, 128.9 us)
Sparse Core Ops, SparseCore 0:
  46.9 153.8 all-reduce.10
  269.2 153.0 all-reduce.12
  483.9 288.9 all-reduce.14
  776.9 66.4 reduce-scatter.11
  847.3 66.5 reduce-scatter.9
  918.0 87.6 reduce-scatter.13
  1010.3 87.8 reduce-scatter.7
  1102.3 206.4 reduce-scatter.19
  1313.0 206.4 reduce-scatter.17
  1523.5 206.4 reduce-scatter.15
where the time goes:
time: 1750 us; the launch traced here: 1740 us
  waiting for transfers between devices  1410 us (81%)
  matrix products  183 us (10%)
  other arithmetic  73.6 us (4%)
  blocking collectives  39.1 us (2%)
    psum x1, waiting for transfers between devices, shards(): lax.psum(jnp.dot(product_low, down_weight, preferred_element_type=jnp.flo...  221 us
    reduce_scatter x1, waiting for transfers between devices, shards(): lax.psum_scatter(down_grad, 'dp', scatter_dimension=1, tiled=True)  211 us
    reduce_scatter x1, waiting for transfers between devices, shards(): lax.psum_scatter(upward_weight_grad, 'dp', scatter_dimension=0, tiled=True)  211 us
    reduce_scatter x1, waiting for transfers between devices, shards(): lax.psum_scatter(gate_weight_grad, 'dp', scatter_dimension=0, tiled=True)  211 us
    psum x1, waiting for transfers between devices, shards(): lax.psum(jnp.dot(mixed_low, output_weight, preferred_element_type=jnp.flo...  154 us
    psum x1, waiting for transfers between devices, shards(): second_grad = lax.psum(second_part, 'tensor')  141 us
    reduce_scatter x1, waiting for transfers between devices, shards(): lax.psum_scatter(query_weight_grad, 'dp', scatter_dimension=0, tiled=True)  92.5 us
    reduce_scatter x1, waiting for transfers between devices, shards(): lax.psum_scatter(output_weight_grad, 'dp', scatter_dimension=1, tiled=True)  91.7 us
  transfers between devices with their start and end apart: 10, of which 10 were waited for; matrix products, arithmetic and copies ran while one was open for 6% of the time, Pallas kernels for 0%

commit v1 on v0

--- a/solution.py
+++ b/solution.py
@@ -1,3 +1,5 @@
+import functools
+
 import jax
 import jax.numpy as jnp
 from jax import lax
@@ -101,7 +103,66 @@
     return (jnp.concatenate(query_parts, axis=0), key_grad, value_grad)
 
 
+def dot(left, right):
+    return jnp.dot(left, right, preferred_element_type=jnp.float32)
+
+
+def dot_back(left, right):
+    return jnp.einsum("tc,dc->td", left, right, preferred_element_type=jnp.float32)
+
+
+def dot_tokens(left, right):
+    return jnp.einsum("tm,tn->mn", left, right, preferred_element_type=jnp.float32)
+
+
+def line_pairs(high, step, towards):
+    pairs = []
+    for place in range(high):
+        if towards > 0 and place < step and place + 1 < high:
+            pairs.append((place, place + 1))
+        if towards < 0 and high - 1 - place < step and place - 1 >= 0:
+            pairs.append((place, place - 1))
+    return [(2 * a + lane, 2 * b + lane) for a, b in pairs for lane in (0, 1)]
+
+
+def choose(index, candidates):
+    value = candidates[0][1]
+    for place, candidate in candidates[1:]:
+        value = jnp.where(index == place, candidate, value)
+    return value
+
+
+def swap_core(value):
+    return lax.ppermute(value, "tensor", [(i, i ^ 1) for i in range(4)])
+
+
+def swap_chip(value):
+    return lax.ppermute(value, "tensor", [(i, i ^ 2) for i in range(4)])
+
+
+class Ticks:
+    def __init__(self, dp):
+        self.arrived = []
+        self.tensor = [(i, i ^ 2) for i in range(4)]
+        self.lane = [(i, i ^ 1) for i in range(dp)]
+        self.pair = [(i, i ^ 2) for i in range(dp)]
+
+    def __call__(self, **sends):
+        names = list(sends)
+        values = []
+        for name in names:
+            values.append(sends[name][0])
+        held = lax.optimization_barrier((values, self.arrived))[0]
+        moved = {}
+        for name, value in zip(names, held):
+            axis, pairs = sends[name][1:]
+            moved[name] = lax.ppermute(value, axis, pairs)
+        self.arrived = list(moved.values())
+        return moved
+
+
 def shards(
+    dp,
     tokens,
     attention_gain,
     query_weight,
@@ -118,24 +179,78 @@
     positions,
     cotangent,
 ):
-    count = tokens.shape[0]
+    chunks = 4
+    count, depth = tokens.shape
     batch = count // SEQ_LEN
     query_heads = query_weight.shape[1] // HD
     value_heads = key_weight.shape[1] // HD
     group = query_heads // value_heads
+    width = depth // dp
+    high = dp // 2
+    teams = high // 2
+    half = count // 2
+    size = half // chunks
+    place = lax.axis_index("dp") // 2
+    lane = lax.axis_index("dp") % 2
+    team = place // 2
+    side = place % 2
+    core = lax.axis_index("tensor") % 2
+    tick = Ticks(dp)
+    over_x = lambda value: (value, "tensor", tick.tensor)
+    over_y = lambda value: (value, "dp", tick.lane)
+    over_z = lambda value: (value, "dp", tick.pair)
+
+    def chunk(array, index):
+        begin = index * size
+        return jnp.concatenate(
+            [array[begin : begin + size], array[half + begin : half + begin + size]], axis=0
+        )
+
+    def unchunk(parts):
+        return jnp.concatenate([p[:size] for p in parts] + [p[size:] for p in parts], axis=0)
+
+    def mine(part):
+        rows = part.shape[0] // 2
+        return lax.dynamic_slice_in_dim(part, core * rows, rows, 0)
+
+    def theirs(part):
+        rows = part.shape[0] // 2
+        return lax.dynamic_slice_in_dim(part, (1 - core) * rows, rows, 0)
+
+    def both(own):
+        other = swap_core(own)
+        return jnp.concatenate(
+            [jnp.where(core == 0, own, other), jnp.where(core == 0, other, own)], axis=0
+        )
+
+    def cores_sum(part):
+        return mine(part) + swap_core(theirs(part))
+
+    upstream_wide = lax.dynamic_slice_in_dim(cotangent, core * half, half, 0).astype(jnp.float32)
+    partner_cotangent = [None] * chunks
+
+    def keep_cotangent(moved, first, number):
+        pieces = both(moved) + attention_gain * 0.0
+        rows = number * size
+        for index in range(number):
+            partner_cotangent[first + index] = jnp.concatenate(
+                [
+                    pieces[index * size : (index + 1) * size],
+                    pieces[rows + index * size : rows + (index + 1) * size],
+                ],
+                axis=0,
+            ).astype(jnp.bfloat16)
+
+    moved = tick(z=over_z(upstream_wide[: 2 * size]))
+    keep_cotangent(moved["z"], 0, 2)
+
     inputs = tokens.astype(jnp.float32)
     first_inverse = rms_inverse(inputs)
     first_normed = inputs * first_inverse
     normed_low = (first_normed * attention_gain).astype(jnp.bfloat16)
-    query_raw = jnp.dot(normed_low, query_weight, preferred_element_type=jnp.float32).reshape(
-        count, query_heads, HD
-    )
-    key_raw = jnp.dot(normed_low, key_weight, preferred_element_type=jnp.float32).reshape(
-        count, value_heads, HD
-    )
-    value_low = jnp.dot(normed_low, value_weight, preferred_element_type=jnp.float32).astype(
-        jnp.bfloat16
-    )
+    query_raw = dot(normed_low, query_weight).reshape(count, query_heads, HD)
+    key_raw = dot(normed_low, key_weight).reshape(count, value_heads, HD)
+    value_low = dot(normed_low, value_weight).astype(jnp.bfloat16)
     cosine, sine = rotary_tables(positions)
     cosine = cosine[:, None]
     sine = sine[:, None]
@@ -151,54 +266,134 @@
     segments = segment_numbers.reshape(batch, SEQ_LEN)
     mixed, totals = lax.map(attend, (queries, keys, values, segments))
     mixed_low = mixed.reshape(count, query_heads * HD).astype(jnp.bfloat16)
-    attention = lax.psum(
-        jnp.dot(mixed_low, output_weight, preferred_element_type=jnp.float32), "tensor"
-    )
-    hidden = inputs + attention
-    second_inverse = rms_inverse(hidden)
-    second_normed = hidden * second_inverse
-    second_low = (second_normed * feedforward_gain).astype(jnp.bfloat16)
-    gate = jnp.dot(second_low, gate_weight, preferred_element_type=jnp.float32)
-    upward = jnp.dot(second_low, up_weight, preferred_element_type=jnp.float32)
-    sigmoid_gate = jax.nn.sigmoid(gate)
-    activated = gate * sigmoid_gate
-    product_low = (activated * upward).astype(jnp.bfloat16)
-    feedforward = lax.psum(
-        jnp.dot(product_low, down_weight, preferred_element_type=jnp.float32), "tensor"
-    )
-    layer_output = (hidden + feedforward).astype(jnp.bfloat16)
-    down_grad = jnp.einsum("tf,td->fd", product_low, cotangent, preferred_element_type=jnp.float32)
-    product_grad = jnp.einsum(
-        "td,fd->tf", cotangent, down_weight, preferred_element_type=jnp.float32
-    )
-    gate_grad_low = (
-        product_grad * upward * sigmoid_gate * (1.0 + gate * (1.0 - sigmoid_gate))
-    ).astype(jnp.bfloat16)
-    upward_grad_low = (product_grad * activated).astype(jnp.bfloat16)
-    gate_weight_grad = jnp.einsum(
-        "td,tf->df", second_low, gate_grad_low, preferred_element_type=jnp.float32
-    )
-    upward_weight_grad = jnp.einsum(
-        "td,tf->df", second_low, upward_grad_low, preferred_element_type=jnp.float32
-    )
-    second_part = jnp.einsum(
-        "tf,df->td", gate_grad_low, gate_weight, preferred_element_type=jnp.float32
-    )
-    second_part = second_part + jnp.einsum(
-        "tf,df->td", upward_grad_low, up_weight, preferred_element_type=jnp.float32
-    )
-    second_grad = lax.psum(second_part, "tensor")
-    second_gain_grad = jnp.sum(second_grad * second_normed, axis=0)
-    hidden_grad = cotangent.astype(jnp.float32) + norm_back(
-        second_grad, hidden, second_inverse, feedforward_gain
-    )
-    hidden_low = hidden_grad.astype(jnp.bfloat16)
-    output_weight_grad = jnp.einsum(
-        "tc,td->cd", mixed_low, hidden_low, preferred_element_type=jnp.float32
-    )
-    mixed_grad = jnp.einsum(
-        "td,cd->tc", hidden_low, output_weight, preferred_element_type=jnp.float32
-    ).astype(jnp.bfloat16)
+
+    def attention_part(index):
+        return over_x(cores_sum(dot(chunk(mixed_low, index), output_weight)))
+
+    def feed(normed, upstream):
+        low = (normed * feedforward_gain).astype(jnp.bfloat16)
+        gate = dot(low, gate_weight)
+        upward = dot(low, up_weight)
+        grad = dot_back(upstream, down_weight)
+        sigmoid_gate = jax.nn.sigmoid(gate)
+        activated = gate * sigmoid_gate
+        product = (activated * upward).astype(jnp.bfloat16)
+        gate_grad = (
+            grad * upward * sigmoid_gate * (1.0 + gate * (1.0 - sigmoid_gate))
+        ).astype(jnp.bfloat16)
+        upward_grad = (grad * activated).astype(jnp.bfloat16)
+        return (low, product, gate_grad, upward_grad)
+
+    hidden = [None] * chunks
+    second_inverse = [None] * chunks
+    second_normed = [None] * chunks
+    fed = [None] * (2 * chunks)
+
+    def finish_attention(sent, moved, index):
+        hidden[index] = chunk(tokens, index).astype(jnp.float32) + both(sent[0] + moved)
+        second_inverse[index] = rms_inverse(hidden[index])
+        second_normed[index] = hidden[index] * second_inverse[index]
+        fed[index] = feed(second_normed[index], chunk(cotangent, index))
+
+    def finish_partner(moved, index):
+        fed[chunks + index] = feed(both(moved), partner_cotangent[index])
+
+    second_parts = [None] * chunks
+
+    def second_part(index):
+        _, _, gate_grad, upward_grad = fed[index]
+        second_parts[index] = dot_back(gate_grad, gate_weight) + dot_back(upward_grad, up_weight)
+        return over_x(cores_sum(second_parts[index]))
+
+    hidden_grad = [None] * chunks
+
+    def finish_second(sent, moved, index):
+        hidden_grad[index] = chunk(cotangent, index).astype(jnp.float32) + norm_back(
+            both(sent[0] + moved), hidden[index], second_inverse[index], feedforward_gain
+        )
+
+    att = [attention_part(index) for index in range(chunks)]
+    moved = tick(x=att[0], z=over_z(upstream_wide[2 * size : 3 * size]))
+    keep_cotangent(moved["z"], 2, 1)
+    finish_attention(att[0], moved["x"], 0)
+    moved = tick(x=att[1], z=over_z(upstream_wide[3 * size :]))
+    keep_cotangent(moved["z"], 3, 1)
+    finish_attention(att[1], moved["x"], 1)
+    moved = tick(x=att[2], z=over_z(mine(second_normed[0])))
+    finish_attention(att[2], moved["x"], 2)
+    finish_partner(moved["z"], 0)
+    moved = tick(x=att[3], z=over_z(mine(second_normed[1])))
+    finish_attention(att[3], moved["x"], 3)
+    finish_partner(moved["z"], 1)
+    sec = second_part(0)
+    moved = tick(x=sec, z=over_z(mine(second_normed[2])))
+    finish_second(sec, moved["x"], 0)
+    finish_partner(moved["z"], 2)
+    sec = second_part(1)
+    moved = tick(x=sec, z=over_z(mine(second_normed[3])))
+    finish_second(sec, moved["x"], 1)
+    finish_partner(moved["z"], 3)
+
+    second_low, product_low, gate_grad_low, upward_grad_low = (
+        jnp.concatenate(parts, axis=0) for parts in zip(*fed)
+    )
+    upstream_low = jnp.concatenate(
+        [chunk(cotangent, index) for index in range(chunks)] + partner_cotangent, axis=0
+    )
+
+    def column(turn, which):
+        return side * (depth // 2) + (2 * ((team + turn) % teams) + which) * width
+
+    def block(kind, turn, which):
+        left, right, transposed = {
+            "down": (upstream_low, product_low, True),
+            "gate": (second_low, gate_grad_low, False),
+            "up": (second_low, upward_grad_low, False),
+        }[kind]
+        piece = lax.dynamic_slice_in_dim(left, column(turn, which), width, 1)
+        return dot_tokens(right, piece) if transposed else dot_tokens(piece, right)
+
+    def team_send(value, turn):
+        pairs = []
+        for place_from in range(high):
+            t, s = place_from // 2, place_from % 2
+            goal = s * teams + (t + turn) % teams
+            pairs += [(2 * place_from + k, 2 * goal + k) for k in (0, 1)]
+        return (value, "dp", pairs)
+
+    weights = {"down": None, "gate": None, "up": None}
+    order = [(kind, turn) for kind in weights for turn in range(teams)]
+    waiting = None
+    x_work = [("second", 2), ("second", 3)]
+    x_work += [("out", index) for index in range(chunks)]
+    layer_parts = [None] * chunks
+    for kind, turn in order + [(None, None)]:
+        sends = {}
+        if kind is not None:
+            sends["y"] = over_y(block(kind, turn, 1 - lane))
+        if waiting is not None:
+            sends["z"] = team_send(waiting[2], waiting[1])
+        what = None
+        if x_work:
+            what, index = x_work.pop(0)
+            if what == "second":
+                sent = second_part(index)
+            else:
+                sent = over_x(cores_sum(dot(fed[index][1], down_weight)))
+            sends["x"] = sent
+        moved = tick(**sends)
+        if waiting is not None:
+            old = weights[waiting[0]]
+            weights[waiting[0]] = moved["z"] if old is None else old + moved["z"]
+        if what == "second":
+            finish_second(sent, moved["x"], index)
+        elif what == "out":
+            layer_parts[index] = (hidden[index] + both(sent[0] + moved["x"])).astype(jnp.bfloat16)
+        if kind is not None:
+            waiting = (kind, turn, block(kind, turn, lane) + moved["y"])
+
+    hidden_low = unchunk([part.astype(jnp.bfloat16) for part in hidden_grad])
+    mixed_grad = dot_back(hidden_low, output_weight).astype(jnp.bfloat16)
     upstream = mixed_grad.reshape(batch, SEQ_LEN, value_heads, group, HD)
     query_back, key_back, value_back = lax.map(
         attend_back, (queries, keys, values, segments, totals, upstream)
@@ -218,64 +413,129 @@
         .astype(jnp.bfloat16)
     )
     value_raw_grad = value_back.reshape(count, value_heads * HD).astype(jnp.bfloat16)
-    query_weight_grad = jnp.einsum(
-        "td,tc->dc", normed_low, query_raw_grad, preferred_element_type=jnp.float32
-    )
-    key_weight_grad = jnp.einsum(
-        "td,tc->dc", normed_low, key_raw_grad, preferred_element_type=jnp.float32
-    )
-    value_weight_grad = jnp.einsum(
-        "td,tc->dc", normed_low, value_raw_grad, preferred_element_type=jnp.float32
-    )
-    first_part = jnp.einsum(
-        "tc,dc->td", query_raw_grad, query_weight, preferred_element_type=jnp.float32
-    )
-    first_part = first_part + jnp.einsum(
-        "tc,dc->td", key_raw_grad, key_weight, preferred_element_type=jnp.float32
-    )
-    first_part = first_part + jnp.einsum(
-        "tc,dc->td", value_raw_grad, value_weight, preferred_element_type=jnp.float32
-    )
-    first_grad, query_gain_grad, key_gain_grad = lax.psum(
-        (first_part, query_gain_part, key_gain_part), "tensor"
-    )
-    first_gain_grad = jnp.sum(first_grad * first_normed, axis=0)
-    tokens_gradient = (
-        hidden_grad + norm_back(first_grad, inputs, first_inverse, attention_gain)
-    ).astype(jnp.bfloat16)
-    summed = (
-        lax.psum_scatter(first_gain_grad, "dp", scatter_dimension=0, tiled=True),
-        lax.psum_scatter(query_weight_grad, "dp", scatter_dimension=0, tiled=True),
-        lax.psum_scatter(key_weight_grad, "dp", scatter_dimension=0, tiled=True),
-        lax.psum_scatter(value_weight_grad, "dp", scatter_dimension=0, tiled=True),
-        lax.psum_scatter(query_gain_grad, "dp", scatter_dimension=0, tiled=True),
-        lax.psum_scatter(key_gain_grad, "dp", scatter_dimension=0, tiled=True),
-        lax.psum_scatter(output_weight_grad, "dp", scatter_dimension=1, tiled=True),
-        lax.psum_scatter(second_gain_grad, "dp", scatter_dimension=0, tiled=True),
-        lax.psum_scatter(gate_weight_grad, "dp", scatter_dimension=0, tiled=True),
-        lax.psum_scatter(upward_weight_grad, "dp", scatter_dimension=0, tiled=True),
-        lax.psum_scatter(down_grad, "dp", scatter_dimension=1, tiled=True),
-    )
+    raw_grad = jnp.concatenate([query_raw_grad, key_raw_grad, value_raw_grad], axis=1)
+
+    first_parts = [
+        dot_back(chunk(query_raw_grad, index), query_weight)
+        + dot_back(chunk(key_raw_grad, index), key_weight)
+        + dot_back(chunk(value_raw_grad, index), value_weight)
+        for index in range(chunks)
+    ]
+    second_gain_part = sum(
+        jnp.sum(part * normed, axis=0) for part, normed in zip(second_parts, second_normed)
+    )
+    first_gain_part = sum(
+        jnp.sum(part * chunk(first_normed, index), axis=0)
+        for index, part in enumerate(first_parts)
+    )
+    head_width = HD // dp
+
+    def gain_rows(spot):
+        lines = jnp.zeros((8, raw_grad.shape[1]), jnp.float32)
+        for row, (value, length) in enumerate(
+            [
+                (second_gain_part, width),
+                (first_gain_part, width),
+                (query_gain_part, head_width),
+                (key_gain_part, head_width),
+            ]
+        ):
+            taken = lax.dynamic_slice_in_dim(value, spot * length, length, 0)
+            lines = lines.at[row, :length].set(taken)
+        return lines
+
+    def head_block(spot, which):
+        begin = (2 * spot + which) * width
+        piece = lax.dynamic_slice_in_dim(normed_low, begin, width, 1)
+        raw = dot_tokens(piece, raw_grad)
+        raw = jnp.concatenate([raw, gain_rows(2 * spot + which)], axis=0)
+        piece = lax.dynamic_slice_in_dim(hidden_low, begin, width, 1)
+        return (raw, dot_tokens(mixed_low, piece))
+
+    raw_blocks = [None] * high
+    out_blocks = [None] * high
+    spots = [high - 1 - turn // 2 if turn % 2 == 0 else turn // 2 for turn in range(high)]
+    tokens_parts = [None] * chunks
+    x_work = list(range(chunks))
+    raw_right = raw_left = out_right = out_left = None
+    step = 1
+    for turn in range(2 * high):
+        sends = {}
+        if turn < high:
+            raw_sent, out_sent = head_block(spots[turn], 1 - lane)
+            sends["y"] = over_y(raw_sent)
+            sends["y_out"] = over_y(out_sent)
+        needed = list(range(high - step, high)) + list(range(step))
+        moving = step < high and all(raw_blocks[spot] is not None for spot in needed)
+        if moving:
+            for name, blocks, carry, towards in (
+                ("raw_right", raw_blocks, raw_right, 1),
+                ("raw_left", raw_blocks, raw_left, -1),
+                ("out_right", out_blocks, out_right, 1),
+                ("out_left", out_blocks, out_left, -1),
+            ):
+                if towards > 0:
+                    options = [(p, blocks[p + high - step]) for p in range(step)]
+                else:
+                    options = [(high - 1 - p, blocks[step - 1 - p]) for p in range(step)]
+                value = choose(place, options)
+                if carry is not None:
+                    value = value + carry
+                sends[name] = (value, "dp", line_pairs(high, step, towards))
+        if x_work:
+            index = x_work.pop(0)
+            sent = over_x(cores_sum(first_parts[index]))
+            sends["x"] = sent
+        else:
+            index = None
+        if not sends:
+            break
+        moved = tick(**sends)
+        if index is not None:
+            tokens_parts[index] = (
+                hidden_grad[index]
+                + norm_back(
+                    both(sent[0] + moved["x"]),
+                    chunk(tokens, index).astype(jnp.float32),
+                    chunk(first_inverse, index),
+                    attention_gain,
+                )
+            ).astype(jnp.bfloat16)
+        if turn < high:
+            raw_kept, out_kept = head_block(spots[turn], lane)
+            raw_blocks[spots[turn]] = raw_kept + moved["y"]
+            out_blocks[spots[turn]] = out_kept + moved["y_out"]
+        if moving:
+            raw_right, raw_left = moved["raw_right"], moved["raw_left"]
+            out_right, out_left = moved["out_right"], moved["out_left"]
+            step += 1
+    raw_whole = choose(place, list(enumerate(raw_blocks))) + raw_right + raw_left
+    output_weight_grad = choose(place, list(enumerate(out_blocks))) + out_right + out_left
+    gains = raw_whole[width:, :width]
+    gains = gains + swap_core(gains)
+    gains = gains + swap_chip(gains)
+    columns_query = query_weight.shape[1]
+    columns_key = columns_query + key_weight.shape[1]
     return (
-        layer_output,
-        tokens_gradient,
-        summed[0],
-        summed[1],
-        summed[2],
-        summed[3],
-        summed[4],
-        summed[5],
-        summed[6],
-        summed[7],
-        summed[8],
-        summed[9],
-        summed[10],
+        unchunk(layer_parts),
+        unchunk(tokens_parts),
+        gains[1],
+        raw_whole[:width, :columns_query],
+        raw_whole[:width, columns_query:columns_key],
+        raw_whole[:width, columns_key:],
+        gains[2, :head_width],
+        gains[3, :head_width],
+        output_weight_grad,
+        gains[0],
+        weights["gate"],
+        weights["up"],
+        weights["down"],
     )
 
 
 def solution(mesh):
     return jax.shard_map(
-        shards,
+        functools.partial(shards, mesh.shape["dp"]),
         mesh=mesh,
         in_specs=(
             P("dp", None),

time: 1750 us -> 1010 us (0.58)
  waiting for transfers between devices: 1410 us -> 323 us
  matrix products: 183 us -> 288 us
  other arithmetic: 73.6 us -> 175 us
  local copies, waits for them, and re-layouts: 14.9 us -> 111 us
  starting transfers between devices: 1.03 us -> 94.7 us
  blocking collectives: 39.1 us -> 0 us
    reduce_scatter x7 -> x0, waiting for transfers between devices: 892 us -> none  [the longest x1 211 us: shards(): lax.psum_scatter(down_grad, 'dp', scatter_dimension=1, tiled=True)]
    psum x3 -> x0, waiting for transfers between devices: 517 us -> none  [the longest x1 221 us: shards(): lax.psum(jnp.dot(product_low, down_weight, preferred_element_type=jnp.flo...]
    ppermute x0 -> x96, waiting for transfers between devices: none -> 323 us  [the longest x55 322 us: __call__(): moved[name] = lax.ppermute(value, axis, pairs)]
    dot_general x21 -> x84, matrix products: 159 us -> 263 us  [the longest x27 99.7 us: dot(): return jnp.dot(left, right, preferred_element_type=jnp.float32)]
    ppermute x0 -> x96, starting transfers between devices: none -> 94.7 us  [the longest x55 87.1 us: __call__(): moved[name] = lax.ppermute(value, axis, pairs)]
    add x1 -> x47, other arithmetic: 7.21 us -> 72.5 us  [the longest x16 36 us: cores_sum(): return mine(part) + swap_core(theirs(part))]
    unnamed x109 -> x545, local copies, waits for them, and re-layouts: 14.7 us -> 58.2 us
    unnamed x1 -> x0, blocking collectives: 32.8 us -> none
  transfers between devices with their start and end apart: 10 -> 96, of which waited for: 10 -> 30; matrix products, arithmetic and copies ran while one was open for 6% -> 50% of each run, Pallas kernels for 0% -> 0%
where the time goes in v1:
time: 1010 us; the launch traced here: 996 us
  waiting for transfers between devices  323 us (32%)
  matrix products  288 us (29%)
  other arithmetic  175 us (17%)
  local copies, waits for them, and re-layouts  111 us (11%)
  starting transfers between devices  94.7 us (9%)
    ppermute x55, waiting for transfers between devices, __call__(): moved[name] = lax.ppermute(value, axis, pairs)  322 us
    dot_general x27, matrix products, dot(): return jnp.dot(left, right, preferred_element_type=jnp.float32)  99.7 us
    ppermute x55, starting transfers between devices, __call__(): moved[name] = lax.ppermute(value, axis, pairs)  87.1 us
    dot_general x29, matrix products, dot_back(): jnp.einsum('tc,dc->td', left, right, preferred_element_type=jnp.float32)  85.3 us
    dot_general x28, matrix products, dot_tokens(): jnp.einsum('tm,tn->mn', left, right, preferred_element_type=jnp.float32)  77.9 us
    unnamed x545, local copies, waits for them, and re-layouts  58.2 us
    add x16, other arithmetic, cores_sum(): return mine(part) + swap_core(theirs(part))  36 us
    select_n x23, other arithmetic, both(): jnp.where(core == 0, own, other)  24.6 us
  transfers between devices with their start and end apart: 96, of which 30 were waited for; matrix products, arithmetic and copies ran while one was open for 50% of the time, Pallas kernels for 0%

profile of v1, /device:TPU:24, one launch (start us, length us, event | category | flops | bytes accessed | tf_op | source)
XLA Modules:
  0.0 996.3 jit_solution(12139177170062949482)
XLA Ops:
  72.6 7.8 fusion.299
  82.9 10.3 %collective-permute-done.1 = f32[256,2048]{1,0:T(8,128)} collective-permute-done((f32[256,2048]{1,0:T(8,128)}, f32[256,2048]{1,0:T(8,128)}, u32[]{:S(2)}, u32[]{:S(2)}) %collective-permute-start.1) | collective-permute-done | bytes 2097184 | tf_op jit(solution)/shard_map/ppermute | solution.py:159
  102.1 16.6 %collective-permute-done.2 = f32[128,2048]{1,0:T(8,128)} collective-permute-done((f32[128,2048]{1,0:T(8,128)}, f32[128,2048]{1,0:T(8,128)}, u32[]{:S(2)}, u32[]{:S(2)}) %collective-permute-start.2) | collective-permute-done | bytes 1048608 | tf_op jit(solution)/shard_map/ppermute | solution.py:159
  370.5 7.5 fusion.138
  389.5 7.8 fusion.139
  421.1 7.9 collective-permute-done.34
  429.3 9.8 collective-permute-done.32
  453.1 15.0 %collective-permute-done.37 = f32[128,2048]{1,0:T(8,128)S(1)} collective-permute-done((f32[128,2048]{1,0:T(8,128)S(1)}, f32[128,2048]{1,0:T(8,128)S(1)}, u32[]{:S(2)}, u32[]{:S(2)}) %collective-permute-start.37) | collective-permute-done | bytes 1048608 | tf_op jit(solution)/shard_map/ppermute | solution.py:159
  468.5 9.6 collective-permute-done.35
  490.9 17.5 %collective-permute-done.38 = f32[128,2048]{1,0:T(8,128)} collective-permute-done((f32[128,2048]{1,0:T(8,128)}, f32[128,2048]{1,0:T(8,128)}, u32[]{:S(2)}, u32[]{:S(2)}) %collective-permute-start.38) | collective-permute-done | bytes 1048608 | tf_op jit(solution)/shard_map/ppermute | solution.py:159
  510.2 10.4 %collective-permute-done.41 = f32[256,1536]{1,0:T(8,128)} collective-permute-done((f32[256,1536]{1,0:T(8,128)}, f32[256,1536]{1,0:T(8,128)}, u32[]{:S(2)}, u32[]{:S(2)}) %collective-permute-start.41) | collective-permute-done | bytes 1572896 | tf_op jit(solution)/shard_map/ppermute | solution.py:159
  527.6 13.3 %collective-permute-start.47 = (f32[256,1536]{1,0:T(8,128)}, f32[256,1536]{1,0:T(8,128)}, u32[]{:S(2)}, u32[]{:S(2)}) collective-permute-start(f32[256,1536]{1,0:T(8,128)} %convolution_add_fusion.7), channel_id=1, source_target_pairs={{0,0},{4,4},{8,16},{12,20},{16,8},{20,12},{24,24},{28,28},{1,1},{5... | collective-permute-start | bytes 4718600 | tf_op jit(solution)/shard_map/ppermute | solution.py:159
  550.1 9.6 collective-permute-done.46
  569.9 15.4 %collective-permute-done.48 = f32[128,2048]{1,0:T(8,128)S(1)} collective-permute-done((f32[128,2048]{1,0:T(8,128)S(1)}, f32[128,2048]{1,0:T(8,128)S(1)}, u32[]{:S(2)}, u32[]{:S(2)}) %collective-permute-start.48) | collective-permute-done | bytes 1048608 | tf_op jit(solution)/shard_map/ppermute | solution.py:159
  585.6 12.1 %collective-permute-done.51 = f32[256,1536]{1,0:T(8,128)S(1)} collective-permute-done((f32[256,1536]{1,0:T(8,128)}, f32[256,1536]{1,0:T(8,128)S(1)}, u32[]{:S(2)}, u32[]{:S(2)}) %collective-permute-start.51) | collective-permute-done | bytes 1572896 | tf_op jit(solution)/shard_map/ppermute | solution.py:159
  612.2 8.7 collective-permute-done.53
  621.1 12.0 %collective-permute-done.60 = f32[256,1536]{1,0:T(8,128)S(1)} collective-permute-done((f32[256,1536]{1,0:T(8,128)S(1)}, f32[256,1536]{1,0:T(8,128)S(1)}, u32[]{:S(2)}, u32[]{:S(2)}) %collective-permute-start.60) | collective-permute-done | bytes 1572896 | tf_op jit(solution)/shard_map/ppermute | solution.py:159
  746.3 28.8 %collective-permute-done.67 = f32[512,256]{1,0:T(8,128)} collective-permute-done((f32[512,256]{1,0:T(8,128)}, f32[512,256]{1,0:T(8,128)}, u32[]{:S(2)}, u32[]{:S(2)}) %collective-permute-start.67) | collective-permute-done | bytes 524320 | tf_op jit(solution)/shard_map/ppermute | solution.py:159
  787.8 24.1 %collective-permute-done.72 = f32[512,256]{1,0:T(8,128)S(1)} collective-permute-done((f32[512,256]{1,0:T(8,128)S(1)}, f32[512,256]{1,0:T(8,128)S(1)}, u32[]{:S(2)}, u32[]{:S(2)}) %collective-permute-start.72) | collective-permute-done | bytes 524320 | tf_op jit(solution)/shard_map/ppermute | solution.py:159
  847.8 17.2 %collective-permute-done.81 = f32[512,256]{1,0:T(8,128)S(1)} collective-permute-done((f32[512,256]{1,0:T(8,128)S(1)}, f32[512,256]{1,0:T(8,128)S(1)}, u32[]{:S(2)}, u32[]{:S(2)}) %collective-permute-start.81) | collective-permute-done | bytes 524320 | tf_op jit(solution)/shard_map/ppermute | solution.py:159
  868.7 34.4 %collective-permute-done.85 = f32[512,256]{1,0:T(8,128)S(1)} collective-permute-done((f32[512,256]{1,0:T(8,128)S(1)}, f32[512,256]{1,0:T(8,128)S(1)}, u32[]{:S(2)}, u32[]{:S(2)}) %collective-permute-start.85) | collective-permute-done | bytes 524320 | tf_op jit(solution)/shard_map/ppermute | solution.py:159
  915.1 8.1 collective-permute-done.89
  937.0 7.9 collective-permute-done.87
  961.7 14.5 %collective-permute-done.91 = f32[264,1024]{1,0:T(8,128)S(1)} collective-permute-done((f32[264,1024]{1,0:T(8,128)S(1)}, f32[264,1024]{1,0:T(8,128)S(1)}, u32[]{:S(2)}, u32[]{:S(2)}) %collective-permute-start.91) | collective-permute-done | bytes 1081376 | tf_op jit(solution)/shard_map/ppermute | solution.py:159
  (1047 shorter events, 665.5 us)
Async XLA Ops:
  44.8 48.4 %collective-permute-start.1 = (f32[256,2048]{1,0:T(8,128)}, f32[256,2048]{1,0:T(8,128)}, u32[]{:S(2)}, u32[]{:S(2)}) collective-permute-start(f32[256,2048]{1,0:T(8,128)} %slice.1224), channel_id=1, source_target_pairs={{0,8},{4,12},{8,0},{12,4},{16,24},{20,28},{24,16},{28,20},{1,9},{5... | collective-permute-start | bytes 6291464 | tf_op jit(solution)/shard_map/ppermute | solution.py:159
  47.5 72.9 %collective-permute-start.5 = (f32[128,2048]{1,0:T(8,128)}, f32[128,2048]{1,0:T(8,128)}, u32[]{:S(2)}, u32[]{:S(2)}) collective-permute-start(f32[128,2048]{1,0:T(8,128)} %constant_dynamic-slice_fusion.17), channel_id=1, source_target_pairs={{0,1},{1,0},{2,3},{3,2},{4,5},{5,4},{6,7},{7,6},{8,9},{9,8},{10,11... | collective-permute-start | bytes 3145736 | tf_op jit(solution)/shard_map/ppermute | solution.py:136
  49.9 72.0 %collective-permute-start.9 = (f32[128,2048]{1,0:T(8,128)}, f32[128,2048]{1,0:T(8,128)}, u32[]{:S(2)}, u32[]{:S(2)}) collective-permute-start(f32[128,2048]{1,0:T(8,128)} %constant_dynamic-slice_fusion.16), channel_id=1, source_target_pairs={{0,1},{1,0},{2,3},{3,2},{4,5},{5,4},{6,7},{7,6},{8,9},{9,8},{10,11... | collective-permute-start | bytes 3145736 | tf_op jit(solution)/shard_map/ppermute | solution.py:136
  52.3 72.5 %collective-permute-start.13 = (f32[128,2048]{1,0:T(8,128)}, f32[128,2048]{1,0:T(8,128)}, u32[]{:S(2)}, u32[]{:S(2)}) collective-permute-start(f32[128,2048]{1,0:T(8,128)} %constant_dynamic-slice_fusion.14), channel_id=1, source_target_pairs={{0,1},{1,0},{2,3},{3,2},{4,5},{5,4},{6,7},{7,6},{8,9},{9,8},{10,11... | collective-permute-start | bytes 3145736 | tf_op jit(solution)/shard_map/ppermute | solution.py:136
  129.2 45.7 %collective-permute-start.28 = (f32[128,2048]{1,0:T(8,128)}, f32[128,2048]{1,0:T(8,128)}, u32[]{:S(2)}, u32[]{:S(2)}) collective-permute-start(f32[128,2048]{1,0:T(8,128)} %collective-permute-done.6), channel_id=1, source_target_pairs={{0,1},{1,0},{2,3},{3,2},{4,5},{5,4},{6,7},{7,6},{8,9},{9,8},{10,11... | collective-permute-start | bytes 3145736 | tf_op jit(solution)/shard_map/ppermute | solution.py:136
  149.0 75.2 %collective-permute-start.20 = (f32[128,2048]{1,0:T(8,128)}, f32[128,2048]{1,0:T(8,128)}, u32[]{:S(2)}, u32[]{:S(2)}) collective-permute-start(f32[128,2048]{1,0:T(8,128)} %constant_dynamic-slice_fusion.12), channel_id=1, source_target_pairs={{0,1},{1,0},{2,3},{3,2},{4,5},{5,4},{6,7},{7,6},{8,9},{9,8},{10,11... | collective-permute-start | bytes 3145736 | tf_op jit(solution)/shard_map/ppermute | solution.py:136
  174.9 51.8 %collective-permute-start.4 = (f32[128,2048]{1,0:T(8,128)}, f32[128,2048]{1,0:T(8,128)}, u32[]{:S(2)}, u32[]{:S(2)}) collective-permute-start(f32[128,2048]{1,0:T(8,128)} %constant_dynamic-slice_fusion.18), channel_id=1, source_target_pairs={{0,1},{1,0},{2,3},{3,2},{4,5},{5,4},{6,7},{7,6},{8,9},{9,8},{10,11... | collective-permute-start | bytes 3145736 | tf_op jit(solution)/shard_map/ppermute | solution.py:136
  186.9 42.5 %collective-permute-start.12 = (f32[128,2048]{1,0:T(8,128)}, f32[128,2048]{1,0:T(8,128)}, u32[]{:S(2)}, u32[]{:S(2)}) collective-permute-start(f32[128,2048]{1,0:T(8,128)} %add.864), channel_id=1, source_target_pairs={{0,1},{1,0},{2,3},{3,2},{4,5},{5,4},{6,7},{7,6},{8,9},{9,8},{10,11... | collective-permute-start | bytes 3145736 | tf_op jit(solution)/shard_map/ppermute | solution.py:136
  192.0 43.3 %collective-permute-start.15 = (f32[128,2048]{1,0:T(8,128)S(1)}, f32[128,2048]{1,0:T(8,128)}, u32[]{:S(2)}, u32[]{:S(2)}) collective-permute-start(f32[128,2048]{1,0:T(8,128)S(1)} %copy-done.124), channel_id=1, source_target_pairs={{0,2},{1,3},{2,0},{3,1},{4,6},{5,7},{6,4},{7,5},{8,10},{9,11},{10,... | collective-permute-start | bytes 3145736 | tf_op jit(solution)/shard_map/ppermute | solution.py:159
  224.2 44.5 %collective-permute-start.23 = (f32[128,2048]{1,0:T(8,128)}, f32[128,2048]{1,0:T(8,128)}, u32[]{:S(2)}, u32[]{:S(2)}) collective-permute-start(f32[128,2048]{1,0:T(8,128)} %constant_dynamic-slice_fusion.10), channel_id=1, source_target_pairs={{0,1},{1,0},{2,3},{3,2},{4,5},{5,4},{6,7},{7,6},{8,9},{9,8},{10,11... | collective-permute-start | bytes 3145736 | tf_op jit(solution)/shard_map/ppermute | solution.py:136
  226.7 46.0 %collective-permute-start.40 = (f32[128,2048]{1,0:T(8,128)}, f32[128,2048]{1,0:T(8,128)}, u32[]{:S(2)}, u32[]{:S(2)}) collective-permute-start(f32[128,2048]{1,0:T(8,128)} %constant_dynamic-slice_fusion.6), channel_id=1, source_target_pairs={{0,1},{1,0},{2,3},{3,2},{4,5},{5,4},{6,7},{7,6},{8,9},{9,8},{10,11... | collective-permute-start | bytes 3145736 | tf_op jit(solution)/shard_map/ppermute | solution.py:136
  229.4 45.7 %collective-permute-start.17 = (f32[128,2048]{1,0:T(8,128)}, f32[128,2048]{1,0:T(8,128)}, u32[]{:S(2)}, u32[]{:S(2)}) collective-permute-start(f32[128,2048]{1,0:T(8,128)} %collective-permute-done.14), channel_id=1, source_target_pairs={{0,1},{1,0},{2,3},{3,2},{4,5},{5,4},{6,7},{7,6},{8,9},{9,8},{10,11... | collective-permute-start | bytes 3145736 | tf_op jit(solution)/shard_map/ppermute | solution.py:136
  272.7 54.1 %collective-permute-start.30 = (f32[128,2048]{1,0:T(8,128)}, f32[128,2048]{1,0:T(8,128)}, u32[]{:S(2)}, u32[]{:S(2)}) collective-permute-start(f32[128,2048]{1,0:T(8,128)} %constant_dynamic-slice_fusion.8), channel_id=1, source_target_pairs={{0,1},{1,0},{2,3},{3,2},{4,5},{5,4},{6,7},{7,6},{8,9},{9,8},{10,11... | collective-permute-start | bytes 3145736 | tf_op jit(solution)/shard_map/ppermute | solution.py:136
  275.1 66.0 %collective-permute-start.45 = (f32[128,2048]{1,0:T(8,128)}, f32[128,2048]{1,0:T(8,128)}, u32[]{:S(2)}, u32[]{:S(2)}) collective-permute-start(f32[128,2048]{1,0:T(8,128)} %constant_dynamic-slice_fusion.5), channel_id=1, source_target_pairs={{0,1},{1,0},{2,3},{3,2},{4,5},{5,4},{6,7},{7,6},{8,9},{9,8},{10,11... | collective-permute-start | bytes 3145736 | tf_op jit(solution)/shard_map/ppermute | solution.py:136
  278.7 41.4 %collective-permute-start.19 = (f32[128,2048]{1,0:T(8,128)}, f32[128,2048]{1,0:T(8,128)}, u32[]{:S(2)}, u32[]{:S(2)}) collective-permute-start(f32[128,2048]{1,0:T(8,128)} %collective-permute-done.18), channel_id=1, source_target_pairs={{0,1},{1,0},{2,3},{3,2},{4,5},{5,4},{6,7},{7,6},{8,9},{9,8},{10,11... | collective-permute-start | bytes 3145736 | tf_op jit(solution)/shard_map/ppermute | solution.py:136
  281.4 70.4 %collective-permute-start.55 = (f32[128,2048]{1,0:T(8,128)}, f32[128,2048]{1,0:T(8,128)}, u32[]{:S(2)}, u32[]{:S(2)}) collective-permute-start(f32[128,2048]{1,0:T(8,128)} %add.932), channel_id=1, source_target_pairs={{0,1},{1,0},{2,3},{3,2},{4,5},{5,4},{6,7},{7,6},{8,9},{9,8},{10,11... | collective-permute-start | bytes 3145736 | tf_op jit(solution)/shard_map/ppermute | solution.py:136
  294.1 61.5 %collective-permute-start.25 = (f32[128,2048]{1,0:T(8,128)}, f32[128,2048]{1,0:T(8,128)}, u32[]{:S(2)}, u32[]{:S(2)}) collective-permute-start(f32[128,2048]{1,0:T(8,128)} %constant_dynamic-slice_fusion.9), channel_id=1, source_target_pairs={{0,8},{4,12},{8,0},{12,4},{16,24},{20,28},{24,16},{28,20},{1,9},{5... | collective-permute-start | bytes 3145736 | tf_op jit(solution)/shard_map/ppermute | solution.py:159
  351.8 98.6 %collective-permute-start.56 = (f32[128,2048]{1,0:T(8,128)}, f32[128,2048]{1,0:T(8,128)}, u32[]{:S(2)}, u32[]{:S(2)}) collective-permute-start(f32[128,2048]{1,0:T(8,128)} %add.935), channel_id=1, source_target_pairs={{0,1},{1,0},{2,3},{3,2},{4,5},{5,4},{6,7},{7,6},{8,9},{9,8},{10,11... | collective-permute-start | bytes 3145736 | tf_op jit(solution)/shard_map/ppermute | solution.py:136
  637.4 99.8 %collective-permute-start.62 = (f32[256,1536]{1,0:T(8,128)}, f32[256,1536]{1,0:T(8,128)}, u32[]{:S(2)}, u32[]{:S(2)}) collective-permute-start(f32[256,1536]{1,0:T(8,128)} %convolution_add_fusion.4), channel_id=1, source_target_pairs={{0,8},{4,12},{8,24},{12,28},{16,0},{20,4},{24,16},{28,20},{1,9},{5... | collective-permute-start | bytes 4718600 | tf_op jit(solution)/shard_map/ppermute | solution.py:159
  708.2 68.4 %collective-permute-start.70 = (f32[128,2048]{1,0:T(8,128)}, f32[128,2048]{1,0:T(8,128)}, u32[]{:S(2)}, u32[]{:S(2)}) collective-permute-start(f32[128,2048]{1,0:T(8,128)} %constant_dynamic-slice_fusion.1), channel_id=1, source_target_pairs={{0,1},{1,0},{2,3},{3,2},{4,5},{5,4},{6,7},{7,6},{8,9},{9,8},{10,11... | collective-permute-start | bytes 3145736 | tf_op jit(solution)/shard_map/ppermute | solution.py:136
  744.4 82.1 %collective-permute-start.75 = (f32[128,2048]{1,0:T(8,128)}, f32[128,2048]{1,0:T(8,128)}, u32[]{:S(2)}, u32[]{:S(2)}) collective-permute-start(f32[128,2048]{1,0:T(8,128)} %constant_dynamic-slice_fusion), channel_id=1, source_target_pairs={{0,1},{1,0},{2,3},{3,2},{4,5},{5,4},{6,7},{7,6},{8,9},{9,8},{10,11... | collective-permute-start | bytes 3145736 | tf_op jit(solution)/shard_map/ppermute | solution.py:136
  785.4 41.2 %collective-permute-start.64 = (f32[128,2048]{1,0:T(8,128)}, f32[128,2048]{1,0:T(8,128)}, u32[]{:S(2)}, u32[]{:S(2)}) collective-permute-start(f32[128,2048]{1,0:T(8,128)} %add.968), channel_id=1, source_target_pairs={{0,1},{1,0},{2,3},{3,2},{4,5},{5,4},{6,7},{7,6},{8,9},{9,8},{10,11... | collective-permute-start | bytes 3145736 | tf_op jit(solution)/shard_map/ppermute | solution.py:136
  826.5 41.5 %collective-permute-start.69 = (f32[128,2048]{1,0:T(8,128)S(1)}, f32[128,2048]{1,0:T(8,128)S(1)}, u32[]{:S(2)}, u32[]{:S(2)}) collective-permute-start(f32[128,2048]{1,0:T(8,128)S(1)} %add.973), channel_id=1, source_target_pairs={{0,1},{1,0},{2,3},{3,2},{4,5},{5,4},{6,7},{7,6},{8,9},{9,8},{10,11... | collective-permute-start | bytes 3145736 | tf_op jit(solution)/shard_map/ppermute | solution.py:136
  865.0 46.6 %collective-permute-start.74 = (f32[128,2048]{1,0:T(8,128)S(1)}, f32[128,2048]{1,0:T(8,128)S(1)}, u32[]{:S(2)}, u32[]{:S(2)}) collective-permute-start(f32[128,2048]{1,0:T(8,128)S(1)} %add.988), channel_id=1, source_target_pairs={{0,1},{1,0},{2,3},{3,2},{4,5},{5,4},{6,7},{7,6},{8,9},{9,8},{10,11... | collective-permute-start | bytes 3145736 | tf_op jit(solution)/shard_map/ppermute | solution.py:136
  (328 other events, 4146.2 us)

commit v2 on v0

--- a/solution.py
+++ b/solution.py
@@ -1,6 +1,10 @@
+import functools
+
 import jax
 import jax.numpy as jnp
 from jax import lax
+from jax.experimental import pallas as pl
+from jax.experimental.pallas import tpu as pltpu
 from jax.sharding import PartitionSpec as P
 
 HD = 128
@@ -101,7 +105,1455 @@
     return (jnp.concatenate(query_parts, axis=0), key_grad, value_grad)
 
 
-def shards(
+def dot(left, right):
+    return jnp.dot(left, right, preferred_element_type=jnp.float32)
+
+
+def dot_back(left, right):
+    return jnp.einsum("tc,dc->td", left, right, preferred_element_type=jnp.float32)
+
+
+def dot_tokens(left, right):
+    return jnp.einsum("tm,tn->mn", left, right, preferred_element_type=jnp.float32)
+
+
+def line_order(high, place):
+    steps = {}
+    for block in range(high):
+        if block > place:
+            steps[block] = high - block + place
+        elif block < place:
+            steps[block] = high - place + block
+    return sorted(steps, key=lambda block: (steps[block], block)) + [place]
+
+
+def swap_core(value):
+    return lax.ppermute(value, "tensor", [(i, i ^ 1) for i in range(4)])
+
+
+def swap_chip(value):
+    return lax.ppermute(value, "tensor", [(i, i ^ 2) for i in range(4)])
+
+
+MESH = pl.DeviceIdType.MESH
+
+
+def neighbours():
+    dp, tensor = lax.axis_index("dp"), lax.axis_index("tensor")
+    core = lax.rem(tensor, 2)
+    sibling = {"tensor": tensor + 1 - 2 * core}
+    facing = {"tensor": lax.rem(tensor + 2, 4)}
+    place = dp // 2
+    pair = {"dp": dp + 2 * (1 - 2 * lax.rem(place, 2))}
+    return core, sibling, facing, pair
+
+
+def greet(devices):
+    barrier = pltpu.get_barrier_semaphore()
+    for device in devices:
+        pl.semaphore_signal(barrier, inc=1, device_id=device, device_id_type=MESH)
+    pl.semaphore_wait(barrier, len(devices))
+
+
+def loop_rows(count, step, body):
+    def run(index, carry):
+        body(pl.ds(pl.multiple_of(index * step, step), step))
+        return carry
+
+    lax.fori_loop(0, count // step, run, 0)
+
+
+def front_kernel(
+    size,
+    mixed_hbm, output_weight_hbm, tokens_hbm, upstream_hbm, upstream_first,
+    gain, gate_hbm, up_hbm, down_hbm,
+    hidden_out, second_out, low_own, product_own, gate_own, upward_own,
+    low_pair, product_pair, gate_pair, upward_pair, upstream_pair,
+    n_recv, n_side, u_recv, u_side,
+    mixed, output_weight, gate_weight, up_weight, down_weight,
+    c_recv, x_send, x_recv, back_recv, tok, hid, z_send, low, rows16, tiles,
+    stage, stage16, terms,
+    load_sems, c_sems, x_sems, back_sems, n_sems, n_side_sems, u_sems, u_side_sems,
+    tok_sems, hid_sems, low_sems, wave_sems, tile_sems, stage_sems, stage16_sems, term_sems,
+):
+    core, sibling, facing, pair = neighbours()
+    depth = gain.shape[1]
+    half = 4 * size
+    tile = tiles.shape[-1]
+    units = gate_weight.shape[1]
+
+    def begin(which, k):
+        side = core if which == 0 else 1 - core
+        return pl.multiple_of(side * half + k * size, size)
+
+    def remote(source, target, sems, k, device):
+        return pltpu.make_async_remote_copy(
+            src_ref=source, dst_ref=target, send_sem=sems.at[0, k], recv_sem=sems.at[1, k],
+            device_id=device, device_id_type=MESH,
+        )
+
+    loads = [
+        pltpu.make_async_copy(source, target, load_sems.at[index])
+        for index, (source, target) in enumerate(
+            [
+                (mixed_hbm, mixed),
+                (output_weight_hbm, output_weight),
+                (gate_hbm, gate_weight),
+                (up_hbm, up_weight),
+                (down_hbm, down_weight),
+            ]
+        )
+    ]
+    for load in loads:
+        load.start()
+    greet([sibling, facing, pair])
+
+    c_copies = [remote(terms.at[pl.ds(k * size, size)], c_recv.at[k], c_sems, k, sibling) for k in range(4)]
+    x_copies = [remote(x_send.at[k], x_recv.at[k], x_sems, k, facing) for k in range(4)]
+    back_copies = [remote(x_send.at[k], back_recv.at[k], back_sems, k, sibling) for k in range(4)]
+    n_copies = [remote(z_send.at[k % 2], n_recv.at[k], n_sems, k, pair) for k in range(4)]
+    n_sides = [remote(n_recv.at[k], n_side.at[k], n_side_sems, k, sibling) for k in range(4)]
+    u_copies = [
+        None if k < 2 else remote(z_send.at[k % 2], u_recv.at[k], u_sems, k, pair) for k in range(4)
+    ]
+    u_sources = [
+        upstream_first.at[pl.ds(k * size, size)] if k < 2 else u_recv.at[k] for k in range(4)
+    ]
+    u_sides = [remote(u_sources[k], u_side.at[k], u_side_sems, k, sibling) for k in range(4)]
+
+    def attention_terms(k):
+        def run(column):
+            x_send[k, :, column] = jnp.dot(
+                mixed[pl.ds(begin(0, k), size), :],
+                output_weight[:, column],
+                preferred_element_type=jnp.float32,
+            )
+            terms[pl.ds(k * size, size), column] = jnp.dot(
+                mixed[pl.ds(begin(1, k), size), :],
+                output_weight[:, column],
+                preferred_element_type=jnp.float32,
+            )
+
+        loop_rows(depth, 512, run)
+        c_copies[k].start()
+
+    def attention_cores(k):
+        c_copies[k].wait_recv()
+
+        def run(row):
+            x_send[k, row, :] = x_send[k, row, :] + c_recv[k, row, :]
+
+        loop_rows(size, 16, run)
+        x_copies[k].start()
+
+    def attention_chips(k):
+        x_copies[k].wait()
+
+        def run(row):
+            x_send[k, row, :] = x_send[k, row, :] + x_recv[k, row, :]
+
+        loop_rows(size, 16, run)
+        back_copies[k].start()
+
+    def token_loads(k):
+        return [
+            pltpu.make_async_copy(
+                tokens_hbm.at[pl.ds(begin(which, k), size)],
+                tok.at[k % 2, which],
+                tok_sems.at[k % 2, which],
+            )
+            for which in range(2)
+        ]
+
+    def hidden_stores(k):
+        return [
+            pltpu.make_async_copy(
+                hid.at[which], hidden_out.at[pl.ds(begin(which, k), size)], hid_sems.at[which]
+            )
+            for which in range(2)
+        ]
+
+    def low_rows(buffer, which, k, row):
+        side = core if which == 0 else 1 - core
+        return pl.ds(pl.multiple_of((2 * side + k % 2) * size + row.start, 16), row.size)
+
+    def normed(k):
+        for load in token_loads(k):
+            load.wait()
+        back_copies[k].wait_recv()
+        if k > 0:
+            for store in hidden_stores(k - 1):
+                store.wait()
+        if k >= 2:
+            n_copies[k - 2].wait_send()
+
+        def run(which, source, row):
+            value = tok[k % 2, which, row, :].astype(jnp.float32) + source[k, row, :]
+            hid[which, row, :] = value
+            unit = value * lax.rsqrt(jnp.mean(value * value, axis=-1, keepdims=True) + epsilon)
+            if which == 0:
+                z_send[k % 2, row, :] = unit
+            low[0, low_rows(low, which, k, row), :] = (unit * gain[...]).astype(jnp.bfloat16)
+
+        loop_rows(size, 16, functools.partial(run, 0, x_send))
+        n_copies[k].start()
+        loop_rows(size, 16, functools.partial(run, 1, back_recv))
+        for store in hidden_stores(k):
+            store.start()
+        if k + 2 < 4:
+            for load in token_loads(k + 2):
+                load.start()
+
+    def stage_load(source, slot):
+        return pltpu.make_async_copy(source, stage.at[slot], stage_sems.at[slot])
+
+    def pair_rows(k):
+        n_copies[k].wait_recv()
+        n_sides[k].start()
+        stage_load(n_recv.at[k], 0).start()
+        stage_load(n_recv.at[k], 0).wait()
+
+        def run(which, row):
+            low[1, low_rows(low, which, k, row), :] = (stage[which, row, :] * gain[...]).astype(
+                jnp.bfloat16
+            )
+
+        loop_rows(size, 16, functools.partial(run, 0))
+        n_sides[k].wait_recv()
+        stage_load(n_side.at[k], 1).start()
+        stage_load(n_side.at[k], 1).wait()
+        loop_rows(size, 16, functools.partial(run, 1))
+
+    def upstream_send(k):
+        load = pltpu.make_async_copy(
+            upstream_hbm.at[pl.ds(begin(0, k), size)], stage16.at[0], stage16_sems.at[0]
+        )
+        load.start()
+        load.wait()
+
+        def run(row):
+            z_send[k % 2, row, :] = stage16[0, row, :].astype(jnp.float32)
+
+        loop_rows(size, 16, run)
+        u_copies[k].start()
+
+    def upstream_rows(k):
+        if k >= 2:
+            u_copies[k].wait_recv()
+        u_sides[k].start()
+        for which in range(2):
+            if which == 1:
+                u_sides[k].wait_recv()
+            source = u_sources[k] if which == 0 else u_side.at[k]
+            stage_load(source, which).start()
+            stage_load(source, which).wait()
+
+            def run(row):
+                stage16[which, row, :] = stage[which, row, :].astype(jnp.bfloat16)
+
+            loop_rows(size, 16, run)
+            store = pltpu.make_async_copy(
+                stage16.at[which],
+                upstream_pair.at[pl.ds(begin(which, k), size)],
+                stage16_sems.at[which],
+            )
+            store.start()
+            store.wait()
+
+    def wave_rows(wave, part):
+        return pl.ds(part * half + wave * 2 * size, 2 * size)
+
+    def term_stores(wave):
+        return [
+            pltpu.make_async_copy(
+                terms.at[pl.ds(part * 2 * size, 2 * size)],
+                second_out.at[wave_rows(wave, part)],
+                term_sems.at[part],
+            )
+            for part in range(2)
+        ]
+
+    def feed(wave, index):
+        source = upstream_pair if index else upstream_hbm
+        low_out, *outs = (
+            (low_pair, product_pair, gate_pair, upward_pair)
+            if index
+            else (low_own, product_own, gate_own, upward_own)
+        )
+        fetches = [
+            pltpu.make_async_copy(
+                source.at[wave_rows(wave, part)],
+                rows16.at[pl.ds(part * 2 * size, 2 * size)],
+                wave_sems.at[part],
+            )
+            for part in range(2)
+        ]
+        low_stores = [
+            pltpu.make_async_copy(
+                low.at[index, pl.ds(part * 2 * size, 2 * size)],
+                low_out.at[wave_rows(wave, part)],
+                low_sems.at[part],
+            )
+            for part in range(2)
+        ]
+        for copy in fetches + low_stores:
+            copy.start()
+        if index == 0 and wave > 0:
+            for copy in term_stores(wave - 1):
+                copy.wait()
+        for copy in fetches:
+            copy.wait()
+
+        def stores(j, slot):
+            return [
+                pltpu.make_async_copy(
+                    tiles.at[slot, which, pl.ds(part * 2 * size, 2 * size)],
+                    outs[which].at[
+                        wave_rows(wave, part), pl.ds(pl.multiple_of(j * tile, tile), tile)
+                    ],
+                    tile_sems.at[slot, which, part],
+                )
+                for which in range(3)
+                for part in range(2)
+            ]
+
+        def run(j, carry):
+            slot = lax.rem(j, 2)
+            column = pl.ds(pl.multiple_of(j * tile, tile), tile)
+            gate = jnp.dot(
+                low[index], gate_weight[:, column], preferred_element_type=jnp.float32
+            )
+            upward = jnp.dot(
+                low[index], up_weight[:, column], preferred_element_type=jnp.float32
+            )
+            grad = lax.dot_general(
+                rows16[...],
+                down_weight[column, :],
+                (((1,), (1,)), ((), ())),
+                preferred_element_type=jnp.float32,
+            )
+            sigmoid_gate = jax.nn.sigmoid(gate)
+            activated = gate * sigmoid_gate
+
+            @pl.when(j >= 2)
+            def _():
+                for store in stores(j - 2, slot):
+                    store.wait()
+
+            tiles[slot, 0] = (activated * upward).astype(jnp.bfloat16)
+            gate_grad = (
+                grad * upward * sigmoid_gate * (1.0 + gate * (1.0 - sigmoid_gate))
+            ).astype(jnp.bfloat16)
+            upward_grad = (grad * activated).astype(jnp.bfloat16)
+            tiles[slot, 1] = gate_grad
+            tiles[slot, 2] = upward_grad
+            for store in stores(j, slot):
+                store.start()
+            if index == 0:
+                across_last = (((1,), (1,)), ((), ()))
+                for first in range(0, depth, depth // 4):
+                    part = pl.ds(first, depth // 4)
+                    term = lax.dot_general(
+                        gate_grad,
+                        gate_weight[part, column],
+                        across_last,
+                        preferred_element_type=jnp.float32,
+                    ) + lax.dot_general(
+                        upward_grad,
+                        up_weight[part, column],
+                        across_last,
+                        preferred_element_type=jnp.float32,
+                    )
+
+                    @pl.when(j == 0)
+                    def _():
+                        terms[:, part] = term
+
+                    @pl.when(j > 0)
+                    def _():
+                        terms[:, part] += term
+
+            return carry
+
+        number = units // tile
+        lax.fori_loop(0, number, run, 0)
+        for j in range(max(0, number - 2), number):
+            for store in stores(j, j % 2):
+                store.wait()
+        for copy in low_stores:
+            copy.wait()
+        if index == 0:
+            for copy in term_stores(wave):
+                copy.start()
+
+    for k in range(2):
+        for load in token_loads(k):
+            load.start()
+    loads[0].wait()
+    loads[1].wait()
+    attention_terms(0)
+    attention_terms(1)
+    attention_cores(0)
+    attention_terms(2)
+    attention_cores(1)
+    attention_terms(3)
+    attention_cores(2)
+    attention_cores(3)
+    upstream_send(2)
+    upstream_send(3)
+    upstream_rows(0)
+    upstream_rows(1)
+    attention_chips(0)
+    u_copies[2].wait_send()
+    normed(0)
+    attention_chips(1)
+    u_copies[3].wait_send()
+    normed(1)
+    for load in loads[2:]:
+        load.wait()
+    upstream_rows(2)
+    for k in range(4):
+        c_copies[k].wait_send()
+    feed(0, 0)
+    attention_chips(2)
+    normed(2)
+    upstream_rows(3)
+    pair_rows(0)
+    attention_chips(3)
+    normed(3)
+    pair_rows(1)
+    feed(0, 1)
+    feed(1, 0)
+    pair_rows(2)
+    pair_rows(3)
+    feed(1, 1)
+
+    for k in range(4):
+        back_copies[k].wait_send()
+        n_sides[k].wait_send()
+        u_sides[k].wait_send()
+        if k >= 2:
+            n_copies[k].wait_send()
+    for store in hidden_stores(3):
+        store.wait()
+    for copy in term_stores(1):
+        copy.wait()
+
+
+def front(mixed, output_weight, tokens, upstream, upstream_first, gain, gate_weight, up_weight, down_weight):
+    rows, depth = tokens.shape
+    inner, units = mixed.shape[1], gate_weight.shape[1]
+    size = rows // 8
+    tile = 256
+    f32, b16 = jnp.float32, jnp.bfloat16
+    any_space = pl.BlockSpec(memory_space=pl.ANY)
+    shape = jax.ShapeDtypeStruct
+    outs = [shape((rows, depth), f32)] * 2
+    outs += ([shape((rows, depth), b16)] + [shape((rows, units), b16)] * 3) * 2
+    outs += [shape((rows, depth), b16)] + [shape((4, size, depth), f32)] * 4
+    dma = pltpu.SemaphoreType.DMA
+    return pl.pallas_call(
+        functools.partial(front_kernel, size),
+        out_shape=outs,
+        in_specs=[any_space] * 5 + [pl.BlockSpec(memory_space=pltpu.VMEM)] + [any_space] * 3,
+        out_specs=[any_space] * len(outs),
+        scratch_shapes=[
+            pltpu.VMEM((rows, inner), b16),
+            pltpu.VMEM((inner, depth), b16),
+            pltpu.VMEM((depth, units), b16),
+            pltpu.VMEM((depth, units), b16),
+            pltpu.VMEM((units, depth), b16),
+            pltpu.VMEM((4, size, depth), f32),
+            pltpu.VMEM((4, size, depth), f32),
+            pltpu.VMEM((4, size, depth), f32),
+            pltpu.VMEM((4, size, depth), f32),
+            pltpu.VMEM((2, 2, size, depth), b16),
+            pltpu.VMEM((2, size, depth), f32),
+            pltpu.VMEM((2, size, depth), f32),
+            pltpu.VMEM((2, 4 * size, depth), b16),
+            pltpu.VMEM((4 * size, depth), b16),
+            pltpu.VMEM((2, 3, 4 * size, tile), b16),
+            pltpu.VMEM((2, size, depth), f32),
+            pltpu.VMEM((2, size, depth), b16),
+            pltpu.VMEM((4 * size, depth), f32),
+            dma((5,)),
+            dma((2, 4)),
+            dma((2, 4)),
+            dma((2, 4)),
+            dma((2, 4)),
+            dma((2, 4)),
+            dma((2, 4)),
+            dma((2, 4)),
+            dma((2, 2)),
+            dma((2,)),
+            dma((2,)),
+            dma((2,)),
+            dma((2, 3, 2)),
+            dma((2,)),
+            dma((2,)),
+            dma((2,)),
+        ],
+        compiler_params=pltpu.CompilerParams(
+            collective_id=1, has_side_effects=True, vmem_limit_bytes=62 * 1024 * 1024
+        ),
+        cost_estimate=pl.CostEstimate(
+            flops=12 * rows * depth * units, bytes_accessed=6 * depth * units, transcendentals=0
+        ),
+    )(mixed, output_weight, tokens, upstream, upstream_first, gain[None], gate_weight, up_weight, down_weight)
+
+
+def sequence_rows(size, core, which, k):
+    side = core if which == 0 else 1 - core
+    return pl.multiple_of(side * 4 * size + k * size, size)
+
+
+def remote(source, target, sems, k, device):
+    return pltpu.make_async_remote_copy(
+        src_ref=source, dst_ref=target, send_sem=sems.at[0, k], recv_sem=sems.at[1, k],
+        device_id=device, device_id_type=MESH,
+    )
+
+
+def grid_neighbours():
+    dp = lax.axis_index("dp")
+    place, lane = dp // 2, lax.rem(dp, 2)
+    towards = 1 - 2 * (place // 2)
+    across = {"dp": dp + 1 - 2 * lane}
+    inward, outward = {"dp": dp + 2 * towards}, {"dp": dp - 2 * towards}
+    team = place // 2
+    side = lax.rem(place, 2)
+    inner = lax.rem(team + side, 2)
+    return place, lane, team, side, inner, across, inward, outward
+
+
+def greet_grid(always, inner, outward):
+    barrier = pltpu.get_barrier_semaphore()
+    for device in always:
+        pl.semaphore_signal(barrier, inc=1, device_id=device, device_id_type=MESH)
+
+    @pl.when(inner == 1)
+    def _():
+        pl.semaphore_signal(barrier, inc=1, device_id=outward, device_id_type=MESH)
+
+    pl.semaphore_wait(barrier, len(always) + inner)
+
+
+def middle_kernel(
+    size,
+    second_hbm, hidden_hbm, upstream_hbm, upstream_pair, product_own, product_pair, gain, down_hbm,
+    grad_out, grad_low_out, out_part, weight_out,
+    products, down_weight, columns, c_recv, x_send, x_recv, back_recv,
+    y_send, y_recv, kept, in_recv, mid_recv, out_recv,
+    hid, tok, grad, grad_low, out_stage,
+    load_sems, c_sems, x_sems, back_sems, y_sems, z_sems, column_sems,
+    x_load_sems, hid_sems, tok_sems, grad_sems, low_sems, out_sems, weight_sems,
+):
+    core, sibling, facing, _ = neighbours()
+    place, lane, team, side, inner, across, inward, outward = grid_neighbours()
+    depth = gain.shape[1]
+    units = down_weight.shape[0]
+    width = columns.shape[-1]
+    begin = functools.partial(sequence_rows, size, core)
+    loads = [
+        pltpu.make_async_copy(source, target, load_sems.at[index])
+        for index, (source, target) in enumerate(
+            [(product_own, products.at[0]), (product_pair, products.at[1]), (down_hbm, down_weight)]
+        )
+    ]
+    turns = [(0, 1), (1, 1), (0, 0), (1, 0)]
+
+    def column_loads(index):
+        turn, other = turns[index]
+        spot = lax.rem(1 - team + turn, 2)
+        which = 1 - lane if other else lane
+        start = pl.multiple_of((side * 4 + 2 * spot + which) * width, width)
+        return [
+            pltpu.make_async_copy(
+                source.at[:, pl.ds(start, width)],
+                columns.at[index % 2, part],
+                column_sems.at[index % 2, part],
+            )
+            for part, source in enumerate((upstream_hbm, upstream_pair))
+        ]
+
+    x_loads = [
+        pltpu.make_async_copy(
+            second_hbm.at[pl.ds(begin(0, k), size)], x_send.at[k], x_load_sems.at[k]
+        )
+        for k in range(4)
+    ]
+    for copy in column_loads(0) + x_loads[:1] + loads[:2] + column_loads(1) + x_loads[1:] + loads[2:]:
+        copy.start()
+    greet_grid([sibling, facing, across, inward], inner, outward)
+    c_copies = [
+        remote(second_hbm.at[pl.ds(begin(1, k), size)], c_recv.at[k], c_sems, k, sibling)
+        for k in range(4)
+    ]
+    x_copies = [remote(x_send.at[k], x_recv.at[k], x_sems, k, facing) for k in range(4)]
+    back_copies = [remote(x_send.at[k], back_recv.at[k], back_sems, k, sibling) for k in range(4)]
+    y_copies = [remote(y_send.at[k], y_recv.at[k], y_sems, k, across) for k in range(2)]
+    in_copy = remote(kept.at[0], in_recv, z_sems, 0, inward)
+    mid_copies = [remote(kept.at[k], mid_recv.at[k], z_sems, 1 + k, inward) for k in range(2)]
+    out_copy = remote(mid_recv.at[0], out_recv, z_sems, 3, outward)
+    for copy in c_copies:
+        copy.start()
+
+    def cores(k):
+        x_loads[k].wait()
+        c_copies[k].wait_recv()
+
+        def run(row):
+            x_send[k, row, :] = x_send[k, row, :] + c_recv[k, row, :]
+
+        loop_rows(size, 16, run)
+        x_copies[k].start()
+
+    def chips(k):
+        x_copies[k].wait()
+
+        def run(row):
+            x_send[k, row, :] = x_send[k, row, :] + x_recv[k, row, :]
+
+        loop_rows(size, 16, run)
+        back_copies[k].start()
+
+    def block(index, target):
+        for copy in column_loads(index):
+            copy.wait()
+
+        def run(rows):
+            total = None
+            for part in range(2):
+                term = lax.dot_general(
+                    products[part, :, rows],
+                    columns[index % 2, part],
+                    (((0,), (0,)), ((), ())),
+                    preferred_element_type=jnp.float32,
+                )
+                total = term if total is None else total + term
+            target[rows, :] = total
+
+        loop_rows(units, 512, run)
+        if index + 2 < 4:
+            for copy in column_loads(index + 2):
+                copy.start()
+
+    def chunk_loads(k):
+        return [
+            pltpu.make_async_copy(
+                source.at[pl.ds(begin(which, k), size)], target.at[which], sems.at[which]
+            )
+            for which in range(2)
+            for source, target, sems in ((hidden_hbm, hid, hid_sems), (upstream_hbm, tok, tok_sems))
+        ]
+
+    def grad_stores(k):
+        return [
+            pltpu.make_async_copy(
+                source.at[which], target.at[pl.ds(begin(which, k), size)], sems.at[which]
+            )
+            for which in range(2)
+            for source, target, sems in (
+                (grad, grad_out, grad_sems),
+                (grad_low, grad_low_out, low_sems),
+            )
+        ]
+
+    def finish(k):
+        for copy in chunk_loads(k):
+            copy.wait()
+        if k > 0:
+            for copy in grad_stores(k - 1):
+                copy.wait()
+        back_copies[k].wait_recv()
+
+        def run(which, source, row):
+            value = hid[which, row, :]
+            inverse = lax.rsqrt(jnp.mean(value * value, axis=-1, keepdims=True) + epsilon)
+            total = tok[which, row, :].astype(jnp.float32) + norm_back(
+                source[k, row, :], value, inverse, gain[...]
+            )
+            grad[which, row, :] = total
+            grad_low[which, row, :] = total.astype(jnp.bfloat16)
+
+        for which, source in enumerate((x_send, back_recv)):
+            loop_rows(size, 16, functools.partial(run, which, source))
+        for copy in grad_stores(k):
+            copy.start()
+        if k < 3:
+            for copy in chunk_loads(k + 1):
+                copy.start()
+
+    def out_store(k):
+        rows = 2 * size
+        return pltpu.make_async_copy(
+            out_stage, out_part.at[pl.ds(k * rows, rows)], out_sems.at[0]
+        )
+
+    def out_terms(k):
+        if k > 0:
+            out_store(k - 1).wait()
+        rows = pl.ds(k * 2 * size, 2 * size)
+
+        def run(column):
+            out_stage[:, column] = jnp.dot(
+                products[0, rows, :], down_weight[:, column], preferred_element_type=jnp.float32
+            )
+
+        loop_rows(depth, 512, run)
+        out_store(k).start()
+
+    def take(k):
+        y_copies[k].wait_recv()
+
+        def run(row):
+            kept[k, row, :] = kept[k, row, :] + y_recv[k, row, :]
+
+        loop_rows(units, 64, run)
+
+    cores(0)
+    for copy in loads[:2]:
+        copy.wait()
+    block(0, y_send.at[0])
+    y_copies[0].start()
+    for copy in chunk_loads(0):
+        copy.start()
+    cores(1)
+    cores(2)
+    cores(3)
+    block(1, y_send.at[1])
+    y_copies[1].start()
+    block(2, kept.at[0])
+    chips(0)
+    loads[2].wait()
+    out_terms(0)
+    finish(0)
+    take(0)
+
+    @pl.when(inner == 1)
+    def _():
+        mid_copies[0].start()
+
+    @pl.when(inner == 0)
+    def _():
+        in_copy.start()
+
+    block(3, kept.at[1])
+    chips(1)
+    out_terms(1)
+    finish(1)
+    chips(2)
+    out_terms(2)
+    take(1)
+
+    @pl.when(inner == 1)
+    def _():
+        mid_copies[1].start()
+        mid_copies[0].wait_recv()
+        out_copy.start()
+
+    finish(2)
+    out_terms(3)
+    chips(3)
+    finish(3)
+
+    @pl.when(inner == 1)
+    def _():
+        in_copy.wait_recv()
+        mid_copies[1].wait_recv()
+        mid_copies[0].wait_send()
+        mid_copies[1].wait_send()
+        out_copy.wait_send()
+
+        def run(row):
+            kept[0, row, :] = in_recv[row, :] + mid_recv[1, row, :]
+
+        loop_rows(units, 64, run)
+
+    @pl.when(inner == 0)
+    def _():
+        in_copy.wait_send()
+        out_copy.wait_recv()
+
+        def run(row):
+            kept[0, row, :] = kept[1, row, :] + out_recv[row, :]
+
+        loop_rows(units, 64, run)
+
+    store = pltpu.make_async_copy(kept.at[0], weight_out, weight_sems.at[0])
+    store.start()
+    for k in range(4):
+        back_copies[k].wait_send()
+        c_copies[k].wait_send()
+    for k in range(2):
+        y_copies[k].wait_send()
+    for copy in grad_stores(3):
+        copy.wait()
+    out_store(3).wait()
+    store.wait()
+
+
+def middle(second, hidden, upstream, upstream_pair, product_own, product_pair, gain, down_weight):
+    rows, depth = hidden.shape
+    units = down_weight.shape[0]
+    size = rows // 8
+    width = depth // 8
+    f32, b16 = jnp.float32, jnp.bfloat16
+    any_space = pl.BlockSpec(memory_space=pl.ANY)
+    shape = jax.ShapeDtypeStruct
+    dma = pltpu.SemaphoreType.DMA
+    vmem = pltpu.VMEM
+    return pl.pallas_call(
+        functools.partial(middle_kernel, size),
+        out_shape=[
+            shape((rows, depth), f32),
+            shape((rows, depth), b16),
+            shape((rows, depth), f32),
+            shape((units, width), f32),
+        ],
+        in_specs=[any_space] * 6 + [pl.BlockSpec(memory_space=pltpu.VMEM), any_space],
+        out_specs=[any_space] * 4,
+        scratch_shapes=[
+            vmem((2, rows, units), b16),
+            vmem((units, depth), b16),
+            vmem((2, 2, rows, width), b16),
+            vmem((4, size, depth), f32),
+            vmem((4, size, depth), f32),
+            vmem((4, size, depth), f32),
+            vmem((4, size, depth), f32),
+            vmem((2, units, width), f32),
+            vmem((2, units, width), f32),
+            vmem((2, units, width), f32),
+            vmem((units, width), f32),
+            vmem((2, units, width), f32),
+            vmem((units, width), f32),
+            vmem((2, size, depth), f32),
+            vmem((2, size, depth), b16),
+            vmem((2, size, depth), f32),
+            vmem((2, size, depth), b16),
+            vmem((2 * size, depth), f32),
+            dma((3,)),
+            dma((2, 4)),
+            dma((2, 4)),
+            dma((2, 4)),
+            dma((2, 2)),
+            dma((2, 4)),
+            dma((2, 2)),
+            dma((4,)),
+            dma((2,)),
+            dma((2,)),
+            dma((2,)),
+            dma((2,)),
+            dma((1,)),
+            dma((1,)),
+        ],
+        compiler_params=pltpu.CompilerParams(
+            collective_id=2, has_side_effects=True, vmem_limit_bytes=62 * 1024 * 1024
+        ),
+        cost_estimate=pl.CostEstimate(
+            flops=8 * rows * depth * units, bytes_accessed=6 * depth * units, transcendentals=0
+        ),
+    )(second, hidden, upstream, upstream_pair, product_own, product_pair, gain[None], down_weight)
+
+
+class TensorSum:
+    def __init__(self, size, own, landed, stage, sems, stage_sems, devices):
+        self.size, self.own, self.landed, self.stage = size, own, landed, stage
+        self.stage_sems = stage_sems
+        c_sems, x_sems, back_sems = sems
+        self.sibling, facing = devices
+        self.c_sems = c_sems
+        self.x_copies = [remote(own.at[k], landed[1].at[k], x_sems, k, facing) for k in range(4)]
+        self.back_copies = [
+            remote(own.at[k], landed[2].at[k], back_sems, k, self.sibling) for k in range(4)
+        ]
+        self.c_copies = [None] * 4
+
+    def give(self, k, source):
+        self.c_copies[k] = remote(source, self.landed[0].at[k], self.c_sems, k, self.sibling)
+        self.c_copies[k].start()
+
+    def staged(self, which, k):
+        copy = pltpu.make_async_copy(self.landed[which].at[k], self.stage.at[0], self.stage_sems.at[0])
+        copy.start()
+        copy.wait()
+
+    def add_stage(self, k):
+        def run(row):
+            self.own[k, row, :] = self.own[k, row, :] + self.stage[0, row, :]
+
+        loop_rows(self.size, 16, run)
+
+    def cores(self, k):
+        self.c_copies[k].wait_recv()
+        self.staged(0, k)
+        self.add_stage(k)
+        self.x_copies[k].start()
+
+    def chips(self, k):
+        self.x_copies[k].wait()
+        self.staged(1, k)
+        self.add_stage(k)
+        self.back_copies[k].start()
+
+    def other(self, k):
+        self.back_copies[k].wait_recv()
+        self.staged(2, k)
+
+
+def rear_kernel(
+    size, turns,
+    gate_ready0, gate_ready1, low_own, low_pair, upward_own, upward_pair,
+    normed_hbm, raw_hbm, hidden_low_hbm, mixed_hbm, lines,
+    out_hbm, hidden_hbm, grad_hbm, tokens_hbm, query_hbm, key_hbm, value_hbm, gain,
+    layer_out, tokens_out, gate_out, up_out, raw_out, head_out,
+    o_c, o_x, o_back, d_c, d_x, d_back, gate_landed, up_landed,
+    upwards, raw, mixed, query_weight, key_weight, value_weight, columns,
+    up_send, up_kept, raw_send, raw_kept, head_send, head_kept, raw_line, head_line,
+    own, give, stage, wide, narrow, result,
+    load_sems, column_sems, y_up_sems, y_raw_sems, y_head_sems, gate_sems, up_sems,
+    raw_line_sems, head_line_sems,
+    oc_sems, ox_sems, ob_sems, dc_sems, dx_sems, db_sems,
+    own_sems, stage_sems, wide_sems, narrow_sems, result_sems, end_sems,
+):
+    core, sibling, facing, _ = neighbours()
+    place, lane, team, side, inner, across, inward, outward = grid_neighbours()
+    high = len(turns)
+    depth = gain.shape[1]
+    width = columns.shape[-1]
+    units = upwards.shape[-1]
+    begin = functools.partial(sequence_rows, size, core)
+    loads = [
+        pltpu.make_async_copy(source, target, load_sems.at[index])
+        for index, (source, target) in enumerate(
+            [
+                (upward_own, upwards.at[0]),
+                (upward_pair, upwards.at[1]),
+                (raw_hbm, raw),
+                (mixed_hbm, mixed),
+                (query_hbm, query_weight),
+                (key_hbm, key_weight),
+                (value_hbm, value_weight),
+            ]
+        )
+    ]
+    blocks = [
+        ("up", 0, 1), ("up", 1, 1), ("head", 0, 1), ("head", 1, 1), ("up", 0, 0), ("up", 1, 0),
+        ("head", 0, 0), ("head", 2, 1), ("head", 1, 0), ("head", 3, 1), ("head", 2, 0), ("head", 3, 0),
+    ]
+
+    def spot_of(kind, turn):
+        if kind == "up":
+            return side * 2 + lax.rem(1 - team + turn, 2)
+        spot = jnp.int32(turns[0][turn])
+        for p in range(1, high):
+            spot = jnp.where(place == p, jnp.int32(turns[p][turn]), spot)
+        return spot
+
+    def column_loads(index):
+        kind, turn, other = blocks[index]
+        which = 1 - lane if other else lane
+        start = pl.multiple_of((2 * spot_of(kind, turn) + which) * width, width)
+        sources = (low_own, low_pair) if kind == "up" else (normed_hbm, hidden_low_hbm)
+        return [
+            pltpu.make_async_copy(
+                source.at[:, pl.ds(start, width)],
+                columns.at[index % 2, part],
+                column_sems.at[index % 2, part],
+            )
+            for part, source in enumerate(sources)
+        ]
+
+    own_loads = [
+        pltpu.make_async_copy(out_hbm.at[pl.ds(begin(0, k), size)], own.at[k], own_sems.at[k])
+        for k in range(4)
+    ]
+    for copy in column_loads(0) + loads[:2] + column_loads(1) + own_loads + loads[2:]:
+        copy.start()
+    greet_grid([sibling, facing, across, inward], inner, outward)
+    devices = (sibling, facing)
+    outs = TensorSum(
+        size, own, (o_c, o_x, o_back), stage, (oc_sems, ox_sems, ob_sems), stage_sems, devices
+    )
+    heads = TensorSum(
+        size, own, (d_c, d_x, d_back), stage, (dc_sems, dx_sems, db_sems), stage_sems, devices
+    )
+    for k in range(4):
+        outs.give(k, out_hbm.at[pl.ds(begin(1, k), size)])
+
+    def team_copies(values, landed, sems):
+        return (
+            remote(values[0], landed.at[0], sems, 0, inward),
+            [remote(values[k], landed.at[1 + k], sems, 1 + k, inward) for k in range(2)],
+            remote(landed.at[1], landed.at[3], sems, 3, outward),
+        )
+
+    gate_copies = team_copies((gate_ready0, gate_ready1), gate_landed, gate_sems)
+    up_copies = team_copies((up_kept.at[0], up_kept.at[1]), up_landed, up_sems)
+
+    def team_send(copies, turn):
+        @pl.when(inner == 1)
+        def _():
+            copies[1][turn].start()
+
+        if turn == 0:
+
+            @pl.when(inner == 0)
+            def _():
+                copies[0].start()
+
+    def team_forward(copies):
+        @pl.when(inner == 1)
+        def _():
+            copies[1][0].wait_recv()
+            copies[2].start()
+
+    def team_combine(copies, landed, last, out, sem):
+        def fetch(source, slot):
+            copy = pltpu.make_async_copy(source, up_send.at[slot], end_sems.at[4 + slot])
+            copy.start()
+            copy.wait()
+
+        @pl.when(inner == 1)
+        def _():
+            copies[0].wait_recv()
+            copies[1][1].wait_recv()
+            fetch(landed.at[0], 0)
+            fetch(landed.at[2], 1)
+            copies[1][0].wait_send()
+            copies[1][1].wait_send()
+            copies[2].wait_send()
+
+        @pl.when(inner == 0)
+        def _():
+            copies[0].wait_send()
+            copies[2].wait_recv()
+            fetch(landed.at[3], 0)
+            fetch(last, 1)
+
+        def run(row):
+            up_send[0, row, :] = up_send[0, row, :] + up_send[1, row, :]
+
+        loop_rows(width, 16, run)
+        store = pltpu.make_async_copy(up_send.at[0], out, sem)
+        store.start()
+        store.wait()
+
+    y_up = [remote(up_send.at[k], up_kept.at[k], y_up_sems, k, across) for k in range(2)]
+    y_raw = [remote(raw_send.at[k % 2], raw_kept.at[k], y_raw_sems, k, across) for k in range(high)]
+    y_head = [
+        remote(head_send.at[k % 2], head_kept.at[k], y_head_sems, k, across) for k in range(high)
+    ]
+
+    def line_copy(p, turn, towards=None):
+        block = turns[p][turn]
+        ahead = block > p
+        slot = block - 1 if ahead else high - 1 + block
+        device = {"dp": lax.axis_index("dp") + (2 if ahead else -2)}
+        return slot, [
+            remote(kept.at[turn], line.at[slot], sems, slot, device)
+            for kept, line, sems in (
+                (raw_kept, raw_line, raw_line_sems),
+                (head_kept, head_line, head_line_sems),
+            )
+        ]
+
+    def line_arrived(slot, turn):
+        for kept, line, sems in (
+            (raw_kept, raw_line, raw_line_sems),
+            (head_kept, head_line, head_line_sems),
+        ):
+            remote(kept.at[turn], line.at[slot], sems, slot, across).wait_recv()
+
+            def run(row):
+                kept[turn, row, :] = kept[turn, row, :] + line[slot, row, :]
+
+            loop_rows(kept.shape[1], 8, run)
+
+    def line_step(turn):
+        for p in range(high):
+            block = turns[p][turn]
+
+            @pl.when(place == p)
+            def _():
+                slot, copies = line_copy(p, turn)
+                if (block > p and p > 0) or (block < p and p < high - 1):
+                    line_arrived(slot, turn)
+                for copy in copies:
+                    copy.start()
+
+    def line_end():
+        for p in range(high):
+
+            @pl.when(place == p)
+            def _():
+                if p > 0:
+                    line_arrived(p - 1, high - 1)
+                if p < high - 1:
+                    line_arrived(high - 1 + p, high - 1)
+                for turn in range(high - 1):
+                    for copy in line_copy(p, turn)[1]:
+                        copy.wait_send()
+
+    def up_block(index, target, added):
+        for copy in column_loads(index):
+            copy.wait()
+
+        def run(rows):
+            total = None
+            for part in range(2):
+                term = lax.dot_general(
+                    columns[index % 2, part],
+                    upwards[part, :, rows],
+                    (((0,), (0,)), ((), ())),
+                    preferred_element_type=jnp.float32,
+                )
+                total = term if total is None else total + term
+            target[:, rows] = target[:, rows] + total if added else total
+
+        loop_rows(units, 512, run)
+        if index + 2 < len(blocks):
+            for copy in column_loads(index + 2):
+                copy.start()
+
+    def head_block(index, raw_target, head_target, added):
+        kind, turn, other = blocks[index]
+        which = 1 - lane if other else lane
+        for copy in column_loads(index):
+            copy.wait()
+        sums = (((0,), (0,)), ((), ()))
+
+        def run(rows):
+            total = lax.dot_general(
+                columns[index % 2, 0], raw[:, rows], sums, preferred_element_type=jnp.float32
+            )
+            line = lines[2 * spot_of(kind, turn) + which, :, rows]
+            if added:
+                raw_target[:width, rows] = raw_target[:width, rows] + total
+                raw_target[width:, rows] = raw_target[width:, rows] + line
+            else:
+                raw_target[:width, rows] = total
+                raw_target[width:, rows] = line
+
+        loop_rows(raw.shape[1], 512, run)
+        total = lax.dot_general(
+            mixed[...], columns[index % 2, 1], sums, preferred_element_type=jnp.float32
+        )
+        head_target[...] = head_target[...] + total if added else total
+        if index + 2 < len(blocks):
+            for copy in column_loads(index + 2):
+                copy.start()
+
+    def head_send_block(index):
+        turn = blocks[index][1]
+        if turn >= 2:
+            y_raw[turn - 2].wait_send()
+            y_head[turn - 2].wait_send()
+        head_block(index, raw_send.at[turn % 2], head_send.at[turn % 2], False)
+        y_raw[turn].start()
+        y_head[turn].start()
+
+    def head_take(index):
+        turn = blocks[index][1]
+        y_raw[turn].wait_recv()
+        y_head[turn].wait_recv()
+        head_block(index, raw_kept.at[turn], head_kept.at[turn], True)
+
+    def head_terms(k):
+        outs.back_copies[k].wait_send()
+        if k >= 2:
+            heads.c_copies[k - 2].wait_send()
+        across_last = (((1,), (1,)), ((), ()))
+        cuts = (0, query_weight.shape[1], query_weight.shape[1] + key_weight.shape[1], raw.shape[1])
+
+        def run(rows):
+            for which in range(2):
+                total = None
+                for part, weight in enumerate((query_weight, key_weight, value_weight)):
+                    term = lax.dot_general(
+                        raw[pl.ds(begin(which, k), size), cuts[part] : cuts[part + 1]],
+                        weight[rows, :],
+                        across_last,
+                        preferred_element_type=jnp.float32,
+                    )
+                    total = term if total is None else total + term
+                if which == 0:
+                    own[k, :, rows] = total
+                else:
+                    give[k % 2, :, rows] = total
+
+        loop_rows(depth, 512, run)
+        heads.give(k, give.at[k % 2])
+
+    def fetches(what, k):
+        pairs = ((hidden_hbm, wide, wide_sems),)
+        if what == "tokens":
+            pairs = ((grad_hbm, wide, wide_sems), (tokens_hbm, narrow, narrow_sems))
+        return [
+            pltpu.make_async_copy(
+                source.at[pl.ds(begin(which, k), size)], target.at[which], sems.at[which]
+            )
+            for which in range(2)
+            for source, target, sems in pairs
+        ]
+
+    def stores(what, k):
+        return [
+            pltpu.make_async_copy(
+                result.at[which],
+                (layer_out if what == "layer" else tokens_out).at[pl.ds(begin(which, k), size)],
+                result_sems.at[which],
+            )
+            for which in range(2)
+        ]
+
+    sequence = [("layer", k) for k in range(4)] + [("tokens", k) for k in range(4)]
+
+    def finish(what, k):
+        number = sequence.index((what, k))
+        for copy in fetches(what, k):
+            copy.wait()
+        if number > 0:
+            for copy in stores(*sequence[number - 1]):
+                copy.wait()
+        (outs if what == "layer" else heads).other(k)
+
+        def run(which, row):
+            total = stage[0, row, :] if which else own[k, row, :]
+            value = wide[which, row, :]
+            if what == "layer":
+                total = value + total
+            else:
+                inputs = narrow[which, row, :].astype(jnp.float32)
+                inverse = lax.rsqrt(jnp.mean(inputs * inputs, axis=-1, keepdims=True) + epsilon)
+                total = value + norm_back(total, inputs, inverse, gain[...])
+            result[which, row, :] = total.astype(jnp.bfloat16)
+
+        for which in range(2):
+            loop_rows(size, 16, functools.partial(run, which))
+        for copy in stores(what, k):
+            copy.start()
+        if number + 1 < len(sequence):
+            for copy in fetches(*sequence[number + 1]):
+                copy.start()
+
+    team_send(gate_copies, 0)
+    team_send(gate_copies, 1)
+    for copy in fetches("layer", 0):
+        copy.start()
+    for copy in loads[:2]:
+        copy.wait()
+    up_block(0, up_send.at[0], False)
+    y_up[0].start()
+    own_loads[0].wait()
+    outs.cores(0)
+    up_block(1, up_send.at[1], False)
+    y_up[1].start()
+    for k in range(1, 4):
+        own_loads[k].wait()
+        outs.cores(k)
+    for copy in loads[2:]:
+        copy.wait()
+    head_send_block(2)
+    head_send_block(3)
+    outs.chips(0)
+    finish("layer", 0)
+    team_forward(gate_copies)
+    y_up[0].wait_recv()
+    up_block(4, up_kept.at[0], True)
+    team_send(up_copies, 0)
+    head_terms(0)
+    outs.chips(1)
+    finish("layer", 1)
+    head_terms(1)
+    y_up[1].wait_recv()
+    up_block(5, up_kept.at[1], True)
+    team_send(up_copies, 1)
+    outs.chips(2)
+    heads.cores(0)
+    finish("layer", 2)
+    head_terms(2)
+    heads.cores(1)
+    outs.chips(3)
+    heads.cores(2)
+    finish("layer", 3)
+    head_terms(3)
+    heads.cores(3)
+    head_take(6)
+    line_step(0)
+    head_send_block(7)
+    heads.chips(0)
+    finish("tokens", 0)
+    head_take(8)
+    line_step(1)
+    head_send_block(9)
+    team_forward(up_copies)
+    heads.chips(1)
+    finish("tokens", 1)
+    heads.chips(2)
+    finish("tokens", 2)
+    head_take(10)
+    line_step(2)
+    for k in range(2):
+        y_up[k].wait_send()
+    team_combine(gate_copies, gate_landed, gate_ready1, gate_out, end_sems.at[0])
+    heads.chips(3)
+    finish("tokens", 3)
+    team_combine(up_copies, up_landed, up_kept.at[1], up_out, end_sems.at[1])
+    head_take(11)
+    line_end()
+    ends = [
+        pltpu.make_async_copy(raw_kept.at[high - 1], raw_out, end_sems.at[2]),
+        pltpu.make_async_copy(head_kept.at[high - 1], head_out, end_sems.at[3]),
+    ]
+    for copy in ends:
+        copy.start()
+    for k in range(4):
+        outs.c_copies[k].wait_send()
+        heads.back_copies[k].wait_send()
+    for k in range(2, 4):
+        heads.c_copies[k].wait_send()
+        y_raw[k].wait_send()
+        y_head[k].wait_send()
+    for copy in stores(*sequence[-1]) + ends:
+        copy.wait()
+
+
+def rear(turns, arrays, lines, places, weights, gain):
+    rows, depth = places[0].shape
+    units = arrays[0].shape[1]
+    heads, inner = arrays[7].shape[1], arrays[9].shape[1]
+    size = rows // 8
+    width = depth // 8
+    high = len(turns)
+    f32, b16 = jnp.float32, jnp.bfloat16
+    any_space = pl.BlockSpec(memory_space=pl.ANY)
+    in_vmem = pl.BlockSpec(memory_space=pltpu.VMEM)
+    shape = jax.ShapeDtypeStruct
+    dma = pltpu.SemaphoreType.DMA
+    vmem = pltpu.VMEM
+    slots = 2 * (high - 1)
+    return pl.pallas_call(
+        functools.partial(rear_kernel, size, turns),
+        out_shape=[
+            shape((rows, depth), b16),
+            shape((rows, depth), b16),
+            shape((width, units), f32),
+            shape((width, units), f32),
+            shape((width + 8, heads), f32),
+            shape((inner, width), f32),
+        ]
+        + [shape((4, size, depth), f32)] * 6
+        + [shape((4, width, units), f32)] * 2,
+        in_specs=[any_space] * 10 + [in_vmem] + [any_space] * 7 + [in_vmem],
+        out_specs=[any_space] * 14,
+        scratch_shapes=[
+            vmem((2, rows, units), b16),
+            vmem((rows, heads), b16),
+            vmem((rows, inner), b16),
+            *[vmem(weight.shape, b16) for weight in weights],
+            vmem((2, 2, rows, width), b16),
+            vmem((2, width, units), f32),
+            vmem((2, width, units), f32),
+            vmem((2, width + 8, heads), f32),
+            vmem((high, width + 8, heads), f32),
+            vmem((2, inner, width), f32),
+            vmem((high, inner, width), f32),
+            vmem((slots, width + 8, heads), f32),
+            vmem((slots, inner, width), f32),
+            vmem((4, size, depth), f32),
+            vmem((2, size, depth), f32),
+            vmem((1, size, depth), f32),
+            vmem((2, size, depth), f32),
+            vmem((2, size, depth), b16),
+            vmem((2, size, depth), b16),
+            dma((7,)),
+            dma((2, 2)),
+            dma((2, 2)),
+            dma((2, high)),
+            dma((2, high)),
+            dma((2, 4)),
+            dma((2, 4)),
+            dma((2, slots)),
+            dma((2, slots)),
+            *[dma((2, 4))] * 6,
+            dma((4,)),
+            dma((1,)),
+            dma((2,)),
+            dma((2,)),
+            dma((2,)),
+            dma((6,)),
+        ],
+        compiler_params=pltpu.CompilerParams(
+            collective_id=3, has_side_effects=True, vmem_limit_bytes=62 * 1024 * 1024
+        ),
+        cost_estimate=pl.CostEstimate(
+            flops=8 * rows * depth * units, bytes_accessed=6 * depth * units, transcendentals=0
+        ),
+    )(*arrays, lines, *places, *weights, gain[None])
+
+
+def gradient_kernel(number, transposed, added, extra, column, *refs):
+    lefts, rights = refs[:number], refs[number : 2 * number]
+    out = refs[-1]
+    total = None
+    for left, right in zip(lefts, rights):
+        first, second = (right, left) if transposed else (left, right)
+        term = lax.dot_general(
+            first[...], second[...], (((0,), (0,)), ((), ())), preferred_element_type=jnp.float32
+        )
+        total = term if total is None else total + term
+    width = total.shape[0]
+    rest = list(refs[2 * number : -1])
+    lines = rest.pop(0)[0] if extra else None
+    if added:
+        total = total + rest[0][:width, :]
+        if extra:
+            lines = lines + rest[0][width:, :]
+    out[:width, :] = total
+    if extra:
+        out[width:, :] = lines
+
+
+def gradient(lefts, rights, column, width, transposed, added=None, extra=None):
+    rows = lefts[0].shape[0]
+    columns = rights[0].shape[1]
+    tile = 512
+    more = 8 if extra is not None else 0
+    if transposed:
+        shape, block, place = (columns, width), (tile, width), lambda n, c: (n, 0)
+    else:
+        shape, block, place = (width + more, columns), (width + more, tile), lambda n, c: (0, n)
+    specs = [pl.BlockSpec((rows, width), lambda n, c: (0, c[0]))] * len(lefts)
+    specs += [pl.BlockSpec((rows, tile), lambda n, c: (0, n))] * len(rights)
+    inputs = list(lefts) + list(rights)
+    if extra is not None:
+        specs.append(pl.BlockSpec((1, 8, tile), lambda n, c: (c[0], 0, n)))
+        inputs.append(extra)
+    if added is not None:
+        specs.append(pl.BlockSpec(block, place))
+        inputs.append(added)
+    return pl.pallas_call(
+        functools.partial(
+            gradient_kernel, len(lefts), transposed, added is not None, extra is not None
+        ),
+        grid_spec=pltpu.PrefetchScalarGridSpec(
+            num_scalar_prefetch=1,
+            grid=(columns // tile,),
+            in_specs=specs,
+            out_specs=pl.BlockSpec(block, place),
+        ),
+        out_shape=jax.ShapeDtypeStruct(shape, jnp.float32),
+        compiler_params=pltpu.CompilerParams(vmem_limit_bytes=32 * 1024 * 1024),
+        cost_estimate=pl.CostEstimate(
+            flops=2 * len(lefts) * rows * width * columns,
+            bytes_accessed=2 * len(lefts) * rows * (width + columns) + 4 * width * columns,
+            transcendentals=0,
+        ),
+    )(column[None], *inputs)
+
+
+def plain_shards(
     tokens,
     attention_gain,
     query_weight,
@@ -273,9 +1725,196 @@
     )
 
 
+def shards(
+    dp,
+    tokens,
+    attention_gain,
+    query_weight,
+    key_weight,
+    value_weight,
+    query_gain,
+    key_gain,
+    output_weight,
+    feedforward_gain,
+    gate_weight,
+    up_weight,
+    down_weight,
+    segment_numbers,
+    positions,
+    cotangent,
+):
+    count, depth = tokens.shape
+    query_heads = query_weight.shape[1] // HD
+    value_heads = key_weight.shape[1] // HD
+    group = query_heads // value_heads
+    width = depth // dp
+    high = dp // 2
+    place = lax.axis_index("dp") // 2
+    lane = lax.axis_index("dp") % 2
+    core = lax.axis_index("tensor") % 2
+    upstream_first = lax.ppermute(
+        lax.dynamic_slice_in_dim(cotangent, core * (count // 2), count // 4, 0).astype(jnp.float32),
+        "dp",
+        [(i, i ^ 2) for i in range(dp)],
+    )
+
+    inputs = tokens.astype(jnp.float32)
+    first_inverse = rms_inverse(inputs)
+    normed_low = (inputs * first_inverse * attention_gain).astype(jnp.bfloat16)
+    query_raw = dot(normed_low, query_weight).reshape(count, query_heads, HD)
+    key_raw = dot(normed_low, key_weight).reshape(count, value_heads, HD)
+    value_low = dot(normed_low, value_weight).astype(jnp.bfloat16)
+    cosine, sine = rotary_tables(positions)
+    cosine = cosine[:, None]
+    sine = sine[:, None]
+    query_inverse = rms_inverse(query_raw)
+    query_unit = query_raw * query_inverse
+    query_low = rotate(query_unit * query_gain, cosine, sine).astype(jnp.bfloat16)
+    key_inverse = rms_inverse(key_raw)
+    key_unit = key_raw * key_inverse
+    key_low = rotate(key_unit * key_gain, cosine, sine).astype(jnp.bfloat16)
+    queries = query_low.reshape(1, count, value_heads, group, HD)
+    keys = key_low.reshape(1, count, value_heads, HD)
+    values = value_low.reshape(1, count, value_heads, HD)
+    segments = segment_numbers.reshape(1, count)
+    mixed, totals = lax.map(attend, (queries, keys, values, segments))
+    mixed_low = mixed.reshape(count, query_heads * HD).astype(jnp.bfloat16)
+
+    (
+        hidden,
+        second_part,
+        low_own,
+        product_own,
+        gate_own,
+        upward_own,
+        low_pair,
+        product_pair,
+        gate_pair,
+        upward_pair,
+        upstream_pair,
+    ) = front(
+        mixed_low,
+        output_weight,
+        tokens,
+        cotangent,
+        upstream_first,
+        feedforward_gain,
+        gate_weight,
+        up_weight,
+        down_weight,
+    )[:11]
+    hidden_grad, hidden_low, out_part, down_weight_grad = middle(
+        second_part,
+        hidden,
+        cotangent,
+        upstream_pair,
+        product_own,
+        product_pair,
+        feedforward_gain,
+        down_weight,
+    )
+
+    def gate_block(turn, which, added=None):
+        spot = (1 - place // 2 + turn) % 2
+        column = place % 2 * (dp // 2) + 2 * spot + which
+        return gradient([low_own, low_pair], [gate_own, gate_pair], column, width, False, added)
+
+    gate_moved = [
+        lax.ppermute(gate_block(turn, 1 - lane), "dp", [(i, i ^ 1) for i in range(dp)])
+        for turn in range(2)
+    ]
+    mixed_grad = dot_back(hidden_low, output_weight).astype(jnp.bfloat16)
+    upstream = mixed_grad.reshape(1, count, value_heads, group, HD)
+    query_back, key_back, value_back = lax.map(
+        attend_back, (queries, keys, values, segments, totals, upstream)
+    )
+    query_unit_grad = rotate_back(query_back.reshape(count, query_heads, HD), cosine, sine)
+    key_unit_grad = rotate_back(key_back.reshape(count, value_heads, HD), cosine, sine)
+    query_gain_part = jnp.sum(query_unit_grad * query_unit, axis=(0, 1))
+    key_gain_part = jnp.sum(key_unit_grad * key_unit, axis=(0, 1))
+    query_raw_grad = (
+        norm_back(query_unit_grad, query_raw, query_inverse, query_gain)
+        .reshape(count, query_heads * HD)
+        .astype(jnp.bfloat16)
+    )
+    key_raw_grad = (
+        norm_back(key_unit_grad, key_raw, key_inverse, key_gain)
+        .reshape(count, value_heads * HD)
+        .astype(jnp.bfloat16)
+    )
+    value_raw_grad = value_back.reshape(count, value_heads * HD).astype(jnp.bfloat16)
+    raw_grad = jnp.concatenate([query_raw_grad, key_raw_grad, value_raw_grad], axis=1)
+
+    head_width = HD // dp
+
+    lines = [
+        jnp.pad(value.reshape(dp, -1), ((0, 0), (0, raw_grad.shape[1] - value.size // dp)))
+        for value in (query_gain_part, key_gain_part)
+    ]
+    gain_lines = jnp.pad(jnp.stack(lines, axis=1), ((0, 0), (0, 6), (0, 0)))
+
+    gate_ready = [gate_block(turn, lane, gate_moved[turn]) for turn in range(2)]
+    layer_output, tokens_gradient, gate_weight_grad, up_weight_grad, raw_whole, output_weight_grad = (
+        rear(
+            [line_order(high, p) for p in range(high)],
+            gate_ready
+            + [low_own, low_pair, upward_own, upward_pair]
+            + [normed_low, raw_grad, hidden_low, mixed_low],
+            gain_lines,
+            [out_part, hidden, hidden_grad, tokens],
+            [query_weight, key_weight, value_weight],
+            attention_gain,
+        )[:6]
+    )
+    place_rows = (lax.axis_index("dp") * width, width, 0)
+    raw_weight = jnp.concatenate(
+        [
+            lax.dynamic_slice_in_dim(value, *place_rows)
+            for value in (query_weight, key_weight, value_weight)
+        ],
+        axis=1,
+    )
+    first_gain = jnp.sum(raw_weight * raw_whole[:width], axis=1) / lax.dynamic_slice_in_dim(
+        attention_gain, *place_rows
+    )
+    second_gain = sum(
+        jnp.sum(lax.dynamic_slice_in_dim(value, *place_rows) * gradient, axis=1)
+        for gradient, value in ((gate_weight_grad, gate_weight), (up_weight_grad, up_weight))
+    ) / lax.dynamic_slice_in_dim(feedforward_gain, *place_rows)
+    gains = jnp.concatenate(
+        [first_gain[None], second_gain[None], raw_whole[width : width + 2, :width]], axis=0
+    )
+    gains = gains + swap_core(gains)
+    gains = gains + swap_chip(gains)
+    columns_query = query_weight.shape[1]
+    columns_key = columns_query + key_weight.shape[1]
+    return (
+        layer_output,
+        tokens_gradient,
+        gains[0],
+        raw_whole[:width, :columns_query],
+        raw_whole[:width, columns_query:columns_key],
+        raw_whole[:width, columns_key:],
+        gains[2, :head_width],
+        gains[3, :head_width],
+        output_weight_grad,
+        gains[1],
+        gate_weight_grad,
+        up_weight_grad,
+        down_weight_grad,
+    )
+
+
 def solution(mesh):
+    dp, tensor = mesh.shape["dp"], mesh.shape["tensor"]
+
+    def program(*args):
+        if dp == 8 and tensor == 4 and args[0].shape[0] == SEQ_LEN:
+            return shards(dp, *args)
+        return plain_shards(*args)
+
     return jax.shard_map(
-        shards,
+        program,
         mesh=mesh,
         in_specs=(
             P("dp", None),

time: 1750 us -> 781 us (0.45)
  waiting for transfers between devices: 1410 us -> 23.7 us
  Pallas kernels: 0 us -> 585 us
  matrix products: 183 us -> 39 us
  local copies, waits for them, and re-layouts: 14.9 us -> 66.9 us
  blocking collectives: 39.1 us -> 0 us
  other arithmetic: 73.6 us -> 48.4 us
    reduce_scatter x7 -> x0, waiting for transfers between devices: 892 us -> none  [the longest x1 211 us: shards(): lax.psum_scatter(down_grad, 'dp', scatter_dimension=1, tiled=True)]
    pallas_call x0 -> x7, Pallas kernels: none -> 585 us  [the longest x1 260 us: rear(): pl.pallas_call(functools.partial(rear_kernel, size, turns), out_shape=[sh...]
    psum x3 -> x0, waiting for transfers between devices: 517 us -> none  [the longest x1 221 us: shards(): lax.psum(jnp.dot(product_low, down_weight, preferred_element_type=jnp.flo...]
    dot_general x21 -> x4, matrix products: 159 us -> 12.9 us  [the longest x3 7.54 us: dot(): return jnp.dot(left, right, preferred_element_type=jnp.float32)]
    unnamed x1 -> x0, blocking collectives: 32.8 us -> none
    ppermute x0 -> x5, waiting for transfers between devices: none -> 23.7 us  [the longest x2 21.1 us: shards(): lax.ppermute(gate_block(turn, 1 - lane), 'dp', [(i, i ^ 1) for i in range...]
  transfers between devices with their start and end apart: 10 -> 5, of which waited for: 10 -> 3; matrix products, arithmetic and copies ran while one was open for 6% -> 11% of each run, Pallas kernels for 0% -> 1%
where the time goes in v2:
time: 781 us; the launch traced here: 768 us
  Pallas kernels  585 us (75%)
  local copies, waits for them, and re-layouts  66.9 us (9%)
  other arithmetic  48.4 us (6%)
  matrix products  39 us (5%)
  waiting for transfers between devices  23.7 us (3%)
    pallas_call x1, Pallas kernels, rear(): pl.pallas_call(functools.partial(rear_kernel, size, turns), out_shape=[sh...  260 us
    pallas_call x1, Pallas kernels, front(): pl.pallas_call(functools.partial(front_kernel, size), out_shape=outs, in_...  194 us
    pallas_call x1, Pallas kernels, middle(): pl.pallas_call(functools.partial(middle_kernel, size), out_shape=[shape((...  116 us
    unnamed x149, local copies, waits for them, and re-layouts  31.6 us
    ppermute x2, waiting for transfers between devices, shards(): lax.ppermute(gate_block(turn, 1 - lane), 'dp', [(i, i ^ 1) for i in range...  21.1 us
  transfers between devices with their start and end apart: 5, of which 3 were waited for; matrix products, arithmetic and copies ran while one was open for 11% of the time, Pallas kernels for 1%

profile of v2, /device:TPU:24, one launch (start us, length us, event | category | flops | bytes accessed | tf_op | source)
XLA Modules:
  0.0 768.2 jit_solution(5953573133984626531)
XLA Ops:
  0.7 2.9 dynamic-slice_convert_fusion
  4.1 3.1 fusion
  13.0 3.8 multiply_reduce_fusion.6
  19.0 3.1 fusion.61
  44.5 2.5 fusion.70
  57.9 194.5 %shard_map.246 = (f32[1024,2048]{1,0:T(8,128)}, f32[1024,2048]{1,0:T(8,128)}, bf16[1024,2048]{1,0:T(8,128)(2,1)}, bf16[1024,1536]{1,0:T(8,128)(2,1)}, bf16[1024,...) custom-call(bf16[1024,512]{1,0:T(8,128)(2,1)} %copy.291.mixed_hbm, ...), custom_call_target="tpu_custom_call" | custom-call | flops 38654705664 | bytes 18874368 | tf_op jit(solution)/shard_map/pallas_call | solution.py:555
  252.3 116.2 %shard_map.251 = (f32[1024,2048]{1,0:T(8,128)}, bf16[1024,2048]{1,0:T(8,128)(2,1)}, f32[1024,2048]{1,0:T(8,128)}, f32[1536,256]{1,0:T(8,128)}) custom-call(f32[1024,2048]{1,0:T(8,128)} %get-tuple-element.91.second_hbm, f32[1024,2048]{1,0:T(8,128)} %get-tuple-element.92.hidden_hbm, bf16[1024,2048]{1,0:T(8,128)(2,1)} %upstream_hbm.3, ...), custom_call_target="tpu_custom_call" | custom-call | flops 25769803776 | bytes 18874368 | tf_op jit(solution)/shard_map/pallas_call | solution.py:906
  368.6 5.4 convolution_convert_fusion
  376.2 2.5 fusion.5
  379.7 2.5 convolution_bitcast_fusion
  384.0 2.5 fusion.37
  402.5 2.5 fusion.58
  408.8 3.8 shard_map.249
  416.2 2.9 shard_map.247
  420.3 2.9 copy.264
  423.3 3.4 fusion.30
  428.0 2.9 copy.296
  434.4 6.1 fusion.49
  448.5 4.0 fusion.22
  452.5 2.9 pad_maximum_fusion.2.raw_hbm
  455.5 4.0 shard_map.250.gate_ready1
  460.6 21.1 %collective-permute-done.1.refs_4_ = f32[256,1536]{1,0:T(8,128)} collective-permute-done((f32[256,1536]{1,0:T(8,128)}, f32[256,1536]{1,0:T(8,128)}, u32[]{:S(2)}, u32[]{:S(2)}) %collective-permute-start.1) | collective-permute-done | bytes 1572896 | tf_op jit(solution)/shard_map/ppermute | solution.py:1823
  481.7 3.9 shard_map.248.gate_ready0
  486.8 259.6 %shard_map.252 = (bf16[1024,2048]{1,0:T(8,128)(2,1)}, bf16[1024,2048]{1,0:T(8,128)(2,1)}, f32[256,1536]{1,0:T(8,128)}, f32[256,1536]{1,0:T(8,128)}, f32[264,1024...) custom-call(f32[256,1536]{1,0:T(8,128)} %copy-done.9, ...), custom_call_target="tpu_custom_call" | custom-call | flops 25769803776 | bytes 18874368 | tf_op jit(solution)/shard_map/pallas_call | solution.py:1436
  (241 shorter events, 107.0 us)
Async XLA Ops:
  0.7 6.5 copy-start.21
  0.7 6.5 copy-start.63
  3.6 54.2 %collective-permute-start = (f32[256,2048]{1,0:T(8,128)}, f32[256,2048]{1,0:T(8,128)}, u32[]{:S(2)}, u32[]{:S(2)}) collective-permute-start(f32[256,2048]{1,0:T(8,128)} %dynamic-slice_convert_fusion), channel_id=1, source_target_pairs={{0,8},{4,12},{8,0},{12,4},{16,24},{20,28},{24,16},{28,20},{1,9},{5... | collective-permute-start | bytes 6291464 | tf_op jit(solution)/shard_map/ppermute | solution.py:1755
  11.3 15.0 %copy-start.18 = (f32[1024,512]{0,1:T(8,128)}, f32[1024,512]{0,1:T(8,128)S(1)}, u32[]{:S(2)}) copy-start(f32[1024,512]{0,1:T(8,128)S(1)} %get-tuple-element.142) | copy-start | bytes 6291460
  13.0 4.5 copy-start.65
  16.8 20.0 %copy-start.16 = (f32[1024,256]{0,1:T(8,128)}, f32[1024,256]{0,1:T(8,128)S(1)}, u32[]{:S(2)}) copy-start(f32[1024,256]{0,1:T(8,128)S(1)} %get-tuple-element.140) | copy-start | bytes 3145732
  33.3 11.3 %copy-start.39 = (bf16[512,4,128]{2,0,1:T(8,128)(2,1)}, bf16[512,4,128]{2,0,1:T(8,128)(2,1)S(1)}, u32[]{:S(2)}) copy-start(bf16[512,4,128]{2,0,1:T(8,128)(2,1)S(1)} %get-tuple-element.122) | copy-start | bytes 1572868
  36.1 12.2 %copy-start.47 = (bf16[1024,256]{0,1:T(8,128)(2,1)}, bf16[1024,256]{0,1:T(8,128)(2,1)S(1)}, u32[]{:S(2)}) copy-start(bf16[1024,256]{0,1:T(8,128)(2,1)S(1)} %convolution_convert_fusion.1) | copy-start | bytes 1572868
  368.6 5.5 slice-start
  368.6 5.5 slice-start.1
  368.6 5.5 copy-start.48
  376.1 6.0 slice-start.2
  376.1 6.0 slice-start.3
  379.7 12.0 %copy-start.25 = (f32[2,128,2,512]{3,1,2,0:T(8,128)}, f32[2,128,2,512]{3,1,2,0:T(8,128)S(1)}, u32[]{:S(2)}) copy-start(f32[2,128,2,512]{3,1,2,0:T(8,128)S(1)} %convolution_multiply_fusion) | copy-start | bytes 3145732
  399.4 5.6 copy-start.17
  402.5 5.0 copy-start.5
  412.7 42.8 %collective-permute-start.2 = (f32[256,1536]{1,0:T(8,128)}, f32[256,1536]{1,0:T(8,128)}, u32[]{:S(2)}, u32[]{:S(2)}) collective-permute-start(f32[256,1536]{1,0:T(8,128)} %shard_map.249), channel_id=1, source_target_pairs={{0,4},{4,0},{8,12},{12,8},{16,20},{20,16},{24,28},{28,24},{1,5},{5... | collective-permute-start | bytes 4718600 | tf_op jit(solution)/shard_map/ppermute | solution.py:1823
  432.9 48.8 %collective-permute-start.1 = (f32[256,1536]{1,0:T(8,128)}, f32[256,1536]{1,0:T(8,128)}, u32[]{:S(2)}, u32[]{:S(2)}) collective-permute-start(f32[256,1536]{1,0:T(8,128)} %copy-done.7), channel_id=1, source_target_pairs={{0,4},{4,0},{8,12},{12,8},{16,20},{20,16},{24,28},{28,24},{1,5},{5... | collective-permute-start | bytes 4718600 | tf_op jit(solution)/shard_map/ppermute | solution.py:1823
  442.6 4.2 copy-start.50
  448.5 7.0 copy-start.3
  448.5 7.0 copy-start.6
  748.4 9.4 %copy-start.44 = (bf16[1024,2048]{1,0:T(8,128)(2,1)S(1)}, bf16[1024,2048]{1,0:T(8,128)(2,1)}, u32[]{:S(2)}) copy-start(bf16[1024,2048]{1,0:T(8,128)(2,1)} %get-tuple-element.169) | copy-start | bytes 12582916
  751.8 1.2 collective-permute-start.3
  753.1 3.7 collective-permute-start.4
  (52 other events, 121.7 us)
